TPU v7x, 32 devices: a whole 2x2x4 slice. The times are simulated.
32 devices in a mesh: groups: 2 (over y), dp: 4 (over z), tensor: 4 (over x, core).
Axes of the slice: x: 2, y: 2, z: 4, core: 2. Of those that a mesh axis runs over, the one named last changes fastest.
Arguments:
- tokens: bfloat16 [4096, 8192], P(('groups', 'dp'), 'tensor'), parts along dimension 0, may hold values from -6 to 6
- norm_gain: float32 [8192], replicated, may hold values from 0.5 to 1.5
- w_inner: bfloat16 [8192, 8192], P('dp', 'tensor'), may hold values from -0.0625 to 0.0625
- w_groups: bfloat16 [8192, 2048], P('dp', 'tensor'), may hold values from -0.0625 to 0.0625
- w_keyval: bfloat16 [8192, 2048], P('dp', 'tensor'), may hold values from -0.0625 to 0.0625
- w_step: bfloat16 [8192, 128], P('dp', 'tensor'), may hold values from -0.0625 to 0.0625
- conv_inner: float32 [4, 8192], P(None, 'tensor'), may hold values from -3 to 3
- conv_groups: float32 [4, 2048], P(None, 'tensor'), may hold values from -3 to 3
- decay_rate: float32 [128], P('tensor'), may hold values from 0.01 to 1
- step_bias: float32 [128], P('tensor'), may hold values from -2 to 0.5
- page_counts: int32 [8, 8], P(('groups', 'dp')), parts along dimension 0, may hold values from 1 to 4, 16 in all within a row
- owners: int32 [64, 1], P(('groups', 'dp')), parts along dimension 0, may hold values from 0 to 3; in each aligned block of 8 rows (0 to 7, 8 to 15, ...) at most 2 rows name the same one
- page_owners: int32 [128, 1], P(('groups', 'dp')), parts along dimension 0, may hold values from 0 to 3; in each aligned block of 16 rows (0 to 15, 16 to 31, ...) at most 4 rows name the same one
Outputs:
- ssm_out: bfloat16 [4096, 8192], P(('groups', 'dp'), 'tensor'), parts along dimension 0
- handed_states: bfloat16 [64, 128, 64, 256], P(('groups', 'dp'), 'tensor'), parts along dimension 0
- handed_tails_inner: bfloat16 [64, 3, 8192], P(('groups', 'dp'), None, 'tensor'), parts along dimension 0
- handed_tails_groups: bfloat16 [64, 3, 2048], P(('groups', 'dp'), None, 'tensor'), parts along dimension 0
- handed_pages: bfloat16 [128, 32, 2048], P(('groups', 'dp'), None, 'tensor'), parts along dimension 0
There are 2 independent parts, one for each index of `groups`. A program takes and returns all parts, laid end to end along the dimension named above; an argument that names none is the same for every part. Nothing has to cross between parts.
Inputs may be any that keep to these rules, and one draw needn't show every extreme that they name: `page_counts`: each request has at least one page; the pages of one index of dp sum to 16. `owners`: at most 2 requests of one index of dp go to one owner. `page_owners`: at most 4 pages of one index of dp go to one owner.
All inputs are finite; a program needn't handle non-finite values.
Results may differ from a plain program's by a relative error of at most 0.0085.
Values may be sent and summed in bfloat16 or wider, within the bound.
A program may use at most 192 MiB of HBM per device.

v0:
```python
import jax
import jax.numpy as jnp
from jax import lax
from jax.sharding import PartitionSpec as P

HEADS = 128
HEAD_DIM = 64
GROUPS = 4
STATE = 256
CAP = 2
PCAP = 4


highest = lax.Precision.HIGHEST


def conv_silu(inputs, kernel, request_of):
    floats = inputs.astype(jnp.float32)
    total = kernel[3] * floats
    for offset in range(1, 4):
        moved = jnp.concatenate(
            [jnp.zeros((offset, floats.shape[1]), jnp.float32), floats[:-offset]], 0
        )
        before = jnp.concatenate([jnp.full((offset,), -1, jnp.int32), request_of[:-offset]], 0)
        total = total + kernel[3 - offset] * jnp.where(
            (before == request_of)[:, None], moved, jnp.float32(0.0)
        )
    return jax.nn.silu(total).astype(jnp.bfloat16)


def request_layout(counts, rows_total, page_rows):
    ends = jnp.cumsum(counts)
    page_of = jnp.arange(rows_total, dtype=jnp.int32) // page_rows
    request_of = jnp.sum((page_of[:, None] >= ends[None, :]).astype(jnp.int32), 1)
    last_rows = ends * page_rows - 1
    return (request_of, last_rows)


def ssd_heads(values, widths, running, keys, queries, request_of, last_rows):
    scores = jnp.dot(queries, keys.T, preferred_element_type=jnp.float32)
    positions = jnp.arange(values.shape[0], dtype=jnp.int32)
    inside = (request_of[:, None] == request_of[None, :]) & (
        positions[None, :] <= positions[:, None]
    )
    gaps = running.T[:, :, None] - running.T[:, None, :]
    decay = jnp.where(
        inside[None], jnp.exp(jnp.where(inside[None], gaps, jnp.float32(0.0))), jnp.float32(0.0)
    )
    mixing = decay * scores[None]
    weighted = widths[:, :, None] * values
    outputs = jnp.einsum("hts,shd->thd", mixing, weighted, precision=highest)
    end_running = running[last_rows]
    requests = jnp.arange(last_rows.shape[0], dtype=jnp.int32)
    member = request_of[None, :] == requests[:, None]
    spans = end_running.T[:, :, None] - running.T[:, None, :]
    reach = jnp.where(
        member[None], jnp.exp(jnp.where(member[None], spans, jnp.float32(0.0))), jnp.float32(0.0)
    )
    states = jnp.einsum(
        "hrs,shd,sn->rhdn", reach, weighted, keys.astype(jnp.float32), precision=highest
    )
    return (outputs, states)


def place_slots(targets, items, owner_count, capacity):
    count = targets.shape[0]
    order = jnp.arange(count, dtype=jnp.int32)
    same = targets[None, :] == targets[:, None]
    earlier = order[None, :] < order[:, None]
    rank = jnp.sum((same & earlier).astype(jnp.int32), 1)
    owner_ids = jnp.arange(owner_count, dtype=jnp.int32)
    slot_ids = jnp.arange(capacity, dtype=jnp.int32)
    picker = (targets[None, None, :] == owner_ids[:, None, None]) & (
        rank[None, None, :] == slot_ids[None, :, None]
    )
    return jnp.einsum(
        "ock,k...->oc...", picker.astype(jnp.bfloat16), items, preferred_element_type=jnp.float32
    ).astype(jnp.bfloat16)


def flatten_slots(received):
    return received.reshape((received.shape[0] * received.shape[1],) + received.shape[2:])


def shards(
    tokens,
    norm_gain,
    w_inner,
    w_groups,
    w_keyval,
    w_step,
    conv_inner,
    conv_groups,
    decay_rate,
    step_bias,
    page_counts,
    owners,
    page_owners,
):
    full_rows = lax.all_gather(tokens, "tensor", axis=1, tiled=True)
    floats = full_rows.astype(jnp.float32)
    scale = lax.rsqrt(jnp.mean(floats * floats, -1, keepdims=True) + 1e-05)
    normed = (floats * scale * norm_gain).astype(jnp.bfloat16)
    joined = jnp.concatenate([w_inner, w_groups, w_keyval], 1)
    rows_here = tokens.shape[0]
    projected = jnp.dot(
        normed, lax.all_gather(joined, "dp", axis=0, tiled=True), preferred_element_type=jnp.float32
    )
    step_sums = jnp.dot(
        normed, lax.all_gather(w_step, "dp", axis=0, tiled=True), preferred_element_type=jnp.float32
    )
    projected = projected.astype(jnp.bfloat16)
    width_inner = w_inner.shape[1]
    width_groups = w_groups.shape[1]
    inner_rows = projected[:, :width_inner]
    group_rows = projected[:, width_inner : width_inner + width_groups]
    keyval = projected[:, width_inner + width_groups :]
    step_rows = step_sums.astype(jnp.bfloat16)
    dp_count = lax.axis_size("dp")
    page_total = page_owners.shape[0]
    page_rows = rows_here // page_total
    request_of, last_rows = request_layout(page_counts[0], rows_here, page_rows)
    pages = keyval.reshape(page_total, page_rows, keyval.shape[1])
    page_send = place_slots(page_owners[:, 0], pages, dp_count, PCAP)
    mixed = conv_silu(inner_rows, conv_inner, request_of)
    grouped_local = conv_silu(group_rows, conv_groups, request_of)
    grouped = lax.all_gather(grouped_local, "tensor", axis=1, tiled=True)
    heads_here = decay_rate.shape[0]
    group_id = lax.axis_index("tensor") * heads_here // (HEADS // GROUPS)
    keys = lax.dynamic_slice_in_dim(grouped, group_id * STATE, STATE, 1)
    queries = lax.dynamic_slice_in_dim(grouped, GROUPS * STATE + group_id * STATE, STATE, 1)
    widths = jax.nn.softplus(step_rows.astype(jnp.float32) + step_bias)
    running = jnp.cumsum(-decay_rate * widths, 0)
    values = mixed.astype(jnp.float32).reshape(rows_here, heads_here, HEAD_DIM)
    outputs, states = ssd_heads(values, widths, running, keys, queries, request_of, last_rows)
    ssm_out = outputs.reshape(rows_here, heads_here * HEAD_DIM).astype(jnp.bfloat16)
    tail_rows = last_rows[:, None] - 2 + jnp.arange(3, dtype=jnp.int32)[None, :]
    targets = owners[:, 0]
    state_send = place_slots(targets, states.astype(jnp.bfloat16), dp_count, CAP)
    inner_send = place_slots(targets, inner_rows[tail_rows], dp_count, CAP)
    group_send = place_slots(targets, group_rows[tail_rows], dp_count, CAP)
    state_received, inner_received, group_received, page_received = (
        lax.all_to_all(state_send, "dp", split_axis=0, concat_axis=0, tiled=True),
        lax.all_to_all(inner_send, "dp", split_axis=0, concat_axis=0, tiled=True),
        lax.all_to_all(group_send, "dp", split_axis=0, concat_axis=0, tiled=True),
        lax.all_to_all(page_send, "dp", split_axis=0, concat_axis=0, tiled=True),
    )
    return (
        ssm_out,
        flatten_slots(state_received),
        flatten_slots(inner_received),
        flatten_slots(group_received),
        flatten_slots(page_received),
    )


def solution(mesh):
    in_specs = (
        P(("groups", "dp"), "tensor"),
        P(),
        P("dp", "tensor"),
        P("dp", "tensor"),
        P("dp", "tensor"),
        P("dp", "tensor"),
        P(None, "tensor"),
        P(None, "tensor"),
        P("tensor"),
        P("tensor"),
        P(("groups", "dp"), None),
        P(("groups", "dp"), None),
        P(("groups", "dp"), None),
    )
    out_specs = (
        P(("groups", "dp"), "tensor"),
        P(("groups", "dp"), "tensor", None, None),
        P(("groups", "dp"), None, "tensor"),
        P(("groups", "dp"), None, "tensor"),
        P(("groups", "dp"), None, "tensor"),
    )
    return jax.shard_map(shards, mesh=mesh, in_specs=in_specs, out_specs=out_specs, check_vma=False)
```

profile of v0, /device:TPU:0, one launch (start us, length us, event | category | flops | bytes accessed | tf_op | source)
XLA Modules:
  0.0 1228.0 jit_solution(3091570774412549398)
XLA Ops:
  7.2 0.7 all-gather.4.cloned.1.call-update
  7.9 0.0 all-gather.6.cloned.1.call-start
  7.9 13.2 %pad_maximum_fusion = bf16[2048,3072]{1,0:T(8,128)(2,1)} fusion(bf16[2048,512]{1,0:T(8,128)(2,1)} %param.17, bf16[2048,512]{1,0:T(8,128)(2,1)} %param.16, bf16[2048,2048]{1,0:T(8,128)(2,1)} %param.15), kind=kLoop, calls=%fused_computation.23 | loop fusion | flops 37748736 | bytes 25165824 | tf_op jit(solution)/shard_map/concatenate | solution.py:104
  21.2 0.0 all-gather.8.cloned.1.call-start
  21.3 0.5 copy-done.24
  21.8 0.2 reduce-window.10
  22.0 0.1 compare_select_fusion.2
  22.1 0.1 reshape.357
  22.2 0.6 pad_clamp_fusion.1
  22.8 0.2 convert_reduce_fusion.2
  22.9 0.2 convert_reduce_fusion.1
  23.1 0.1 convert_reduce_fusion
  23.2 17.5 %all_gather.13 = bf16[8192,32]{0,1:T(8,128)(2,1)S(1)} all-gather(bf16[2048,32]{0,1:T(8,128)(2,1)S(1)} %copy-done.5), channel_id=1, replica_groups=mesh['groups'=2,'dp'=4,'tensor'=4] {'dp'}, dimensions={0}, use_global_device_ids=true | all-gather | bytes 655360 | tf_op jit(solution)/shard_map/all_gather | solution.py:110
  40.8 0.5 iota_compare_fusion.6
  41.3 0.5 iota_compare_fusion.7
  41.8 0.6 iota_compare_fusion.4
  42.4 0.1 add_compare_fusion
  42.5 0.6 iota_compare_fusion.1
  43.1 0.6 fusion.71
  43.7 26.8 %all-gather.4.cloned.1.call-done = bf16[512,8192]{1,0:T(8,128)(2,1)} async-done(((bf16[512,2048]{1,0:T(8,128)(2,1)}), bf16[512,8192]{1,0:T(8,128)(2,1)}) %all-gather.4.cloned.1.call-update) | async-done | bytes 8388624 | tf_op jit(solution)/shard_map/all_gather | solution.py:100
  70.6 5.3 fusion.8
  75.9 0.5 copy-done
  76.3 2.8 compare_select_fusion.1
  79.2 0.1 copy_bitcast_fusion.1
  79.3 1.3 reduce-window.11
  80.6 0.2 slice_reduce_fusion
  80.8 827.4 %all-gather.6.cloned.1.call-done = bf16[8192,3072]{1,0:T(8,128)(2,1)} async-done(((bf16[2048,3072]{1,0:T(8,128)(2,1)}), bf16[8192,3072]{1,0:T(8,128)(2,1)}) %all-gather.6.cloned.1.call-update) | async-done | bytes 50331664 | tf_op jit(solution)/shard_map/all_gather | solution.py:107
  908.2 34.0 %convolution_convert_fusion.1 = bf16[512,3072]{1,0:T(8,128)(2,1)S(1)} fusion(bf16[8192,3072]{1,0:T(8,128)(2,1)} %all-gather.6.cloned.1.call-done, bf16[512,8192]{1,0:T(8,128)(2,1)} %all-gather.4.cloned.1.call-done, f32[8192]{0:T(1024)S(1)} %copy-done.23, f32[512]{0:T(512)S(1)} %add_rsqrt_fusion), kind=kOutput, calls=%fused_computation.27 | convolution fusion | flops 25788153856 | bytes 61900800 | tf_op jit(solution)/shard_map/dot_general | solution.py:106
  942.2 1.2 fusion.69
  943.4 2.1 multiply_convert_fusion.1
  945.5 0.1 copy_bitcast_fusion
  945.6 0.1 copy.76
  945.7 1.3 gather_fusion
  947.0 0.8 copy.77
  947.7 1.7 select_bitcast_fusion
  949.4 2.0 fusion.70
  951.4 6.6 fusion.23
  958.0 5.5 copy.73
  963.5 0.6 gather_fusion.1
  964.2 0.1 reshape.356
  964.2 0.6 gather_fusion.2
  964.9 0.1 convolution_convert_fusion.4
  965.0 0.6 copy.83
  965.7 3.3 all-to-all-start.2
  969.0 1.2 convolution_convert_fusion.3
  970.2 5.1 broadcast_multiply_fusion
  975.3 0.2 convolution_convert_fusion.2
  975.5 0.7 copy.80
  976.2 5.0 all-to-all-start.1
  981.3 19.8 %fusion = bf16[32,64,8,256]{3,2,1,0:T(8,128)(2,1)} fusion(f32[512,32,8]{0,2,1:T(8,128)S(1)} %copy-done.4, f32[512,32,64]{0,2,1:T(8,128)} %broadcast_multiply_fusion, bf16[512,2048]{1,0:T(8,128)(2,1)} %all-gather.8.cloned.1.call-done, s32[]{:T(128)S(6)} %select_n.97), kind=kOutput, calls=%fused_computation.3 | convolution fusion | flops 25778192384 | bytes 13369348 | tf_op jit(solution)/shard_map/hrs,shd,sn->rhdn/dot_general | solution.py:59
  1001.1 5.1 all-to-all-start.3
  1006.2 10.1 convolution_convert_fusion
  1016.2 8.4 copy.78
  1024.7 5.9 all-to-all-start
  1030.6 0.2 fusion.36
  1030.8 0.6 reshape.342
  1031.4 0.1 copy.81
  1031.5 0.7 reshape.341
  1032.2 0.9 copy.86
  1033.1 1.4 fusion.40
  1034.5 39.7 %fusion.24 = bf16[32,64,512]{2,1,0:T(8,128)(2,1)S(1)} fusion(f32[512,32,64]{0,2,1:T(8,128)} %broadcast_multiply_fusion, f32[512,512]{1,0:T(8,128)S(1)} %fusion.40, f32[32,512]{1,0:T(8,128)S(1)} %copy_bitcast_fusion, pred[512,512]{1,0:T(8,128)(4,1)S(1)} %fusion.36), kind=kOutput, calls=%fused_computation.33 | convolution fusion | flops 6477053952 | bytes 7667712 | tf_op jit(solution)/shard_map/hts,shd->thd/dot_general | solution.py:51
  1074.2 2.4 copy.87
  1076.6 136.5 %all-to-all-done = bf16[4,2,32,64,256]{4,3,2,1,0:T(8,128)(2,1)} async-done(((bf16[4,2,32,64,256]{4,3,2,1,0:T(8,128)(2,1)}), bf16[4,2,32,64,256]{4,3,2,1,0:T(8,128)(2,1)}, u32[]{:S(2)}, u32[]{:S(2)}) %all-to-all-start) | async-done | bytes 8388640 | tf_op jit(solution)/shard_map/all_to_all | solution.py:143
  1213.0 8.4 copy.109
  (73 shorter events, 0.3 us)
Async XLA Ops:
  7.2 63.4 %all-gather.4.cloned.1.call-start = ((), (), s32[]{:S(2)}) async-start(), calls=%async_computation.4 | async-start | bytes 10485760 | tf_op jit(solution)/shard_map/all_gather | solution.py:100
  7.9 900.3 %all-gather.6.cloned.1.call-start = ((), (), s32[]{:S(2)}) async-start(), calls=%async_computation.5 | async-start | bytes 62914560 | tf_op jit(solution)/shard_map/all_gather | solution.py:107
  21.1 0.7 copy-start.24
  21.1 0.8 copy-start.25
  21.1 1.6 copy-start.26
  21.1 1.8 copy-start.22
  21.2 2.1 copy-start.5
  21.2 21.9 %copy-start.13 = (f32[4,512]{1,0:T(4,128)S(1)}, f32[4,512]{1,0:T(4,128)}, u32[]{:S(2)}) copy-start(f32[4,512]{1,0:T(4,128)} %param.20) | copy-start | bytes 24580
  21.2 21.9 %copy-start.9 = (f32[4,2048]{1,0:T(4,128)S(1)}, f32[4,2048]{1,0:T(4,128)}, u32[]{:S(2)}) copy-start(f32[4,2048]{1,0:T(4,128)} %param.19) | copy-start | bytes 98308
  21.2 960.0 %all-gather.8.cloned.1.call-start = ((), (), s32[]{:S(2)}) async-start(), calls=%async_computation.6 | async-start | bytes 2621440 | tf_op jit(solution)/shard_map/all_gather | solution.py:127
  42.5 900.9 %copy-start.14 = (pred[512]{0:T(512)(128)(4,1)}, pred[512]{0:T(512)(128)(4,1)S(1)}, u32[]{:S(2)}) copy-start(pred[512]{0:T(512)(128)(4,1)S(1)} %get-tuple-element.43) | copy-start | bytes 1540
  42.5 900.9 %copy-start.16 = (pred[512]{0:T(512)(128)(4,1)}, pred[512]{0:T(512)(128)(4,1)S(1)}, u32[]{:S(2)}) copy-start(pred[512]{0:T(512)(128)(4,1)S(1)} %get-tuple-element.44) | copy-start | bytes 1540
  42.5 900.9 %copy-start.18 = (pred[512]{0:T(512)(128)(4,1)}, pred[512]{0:T(512)(128)(4,1)S(1)}, u32[]{:S(2)}) copy-start(pred[512]{0:T(512)(128)(4,1)S(1)} %get-tuple-element.45) | copy-start | bytes 1540
  43.1 32.8 %copy-start.23 = (f32[8192]{0:T(1024)S(1)}, f32[8192]{0:T(1024)}, u32[]{:S(2)}) copy-start(f32[8192]{0:T(1024)} %param.14) | copy-start | bytes 98308
  43.7 32.1 %copy-start.27 = (f32[32]{0:T(128)S(1)}, f32[32]{0:T(128)}, u32[]{:S(2)}) copy-start(f32[32]{0:T(128)} %param.22) | copy-start | bytes 388
  70.6 5.8 copy-start
  80.8 861.4 %copy-start.10 = (f32[32,5]{0,1:T(8,128)}, f32[32,5]{0,1:T(8,128)S(1)}, u32[]{:S(2)}) copy-start(f32[32,5]{0,1:T(8,128)S(1)} %reduce-window.14) | copy-start | bytes 1924
  943.4 2.1 slice-start
  949.4 2.0 copy-start.6
  949.4 2.0 copy-start.7
  949.4 2.0 copy-start.8
  949.4 2.0 copy-start.15
  949.4 2.0 copy-start.17
  949.4 2.0 copy-start.19
  958.0 5.6 copy-start.1
  958.0 6.3 copy-start.3
  958.0 6.9 copy-start.11
  958.0 6.9 copy-start.12
  958.0 11.0 copy-start.2
  958.0 11.0 copy-start.20
  958.0 11.0 copy-start.21
  965.7 10.5 all-to-all-start.2
  970.2 11.0 copy-start.4
  976.2 24.9 %all-to-all-start.1 = ((bf16[4,2,3,2048]{3,1,2,0:T(2,128)(2,1)}), bf16[4,2,3,2048]{3,1,2,0:T(2,128)(2,1)S(1)}, u32[]{:S(2)}, u32[]{:S(2)}) async-start(bf16[4,2,3,2048]{3,1,2,0:T(2,128)(2,1)} %copy.80), calls=%async_computation.1 | async-start | bytes 196608 | tf_op jit(solution)/shard_map/all_to_all | solution.py:144
  1001.1 23.6 %all-to-all-start.3 = ((bf16[4,4,32,512]{3,1,2,0:T(4,128)(2,1)}), bf16[4,4,32,512]{3,1,2,0:T(4,128)(2,1)S(1)}, u32[]{:S(2)}, u32[]{:S(2)}) async-start(bf16[4,4,32,512]{3,1,2,0:T(4,128)(2,1)} %convolution_convert_fusion.3), calls=%async_computation.3 | async-start | bytes 1048576 | tf_op jit(solution)/shard_map/all_to_all | solution.py:146
  1024.7 188.4 %all-to-all-start = ((bf16[4,2,32,64,256]{4,3,2,1,0:T(8,128)(2,1)}), bf16[4,2,32,64,256]{4,3,2,1,0:T(8,128)(2,1)}, u32[]{:S(2)}, u32[]{:S(2)}) async-start(bf16[4,2,32,64,256]{4,3,2,1,0:T(8,128)(2,1)} %copy.78), calls=%async_computation | async-start | bytes 16777216 | tf_op jit(solution)/shard_map/all_to_all | solution.py:143
Sparse Core Ops, SparseCore 0:
  9.6 60.9 all-gather.3
  72.2 836.0 all-gather.5
  945.6 20.8 all-gather.7
where the time goes:
time: 1230 us
  waiting for transfers between devices  991 us (81%)
  matrix products  109 us (9%)
  other arithmetic  42.3 us (3%)
  local copies, waits for them, and re-layouts  33.9 us (3%)
  starting transfers between devices  19.4 us (2%)
  blocking collectives  17.5 us (1%)
  between operations  14.1 us (1%)
    all_gather x1, waiting for transfers between devices, shards(): lax.all_gather(joined, 'dp', axis=0, tiled=True)  827 us
    all_to_all x1, waiting for transfers between devices, shards(): lax.all_to_all(state_send, 'dp', split_axis=0, concat_axis=0, tiled=True)  136 us
    dot_general x1, matrix products, ssd_heads(): outputs = jnp.einsum('hts,shd->thd', mixing, weighted, precision=highest)  39.7 us
    dot_general x1, matrix products, shards(): jnp.dot(normed, lax.all_gather(joined, 'dp', axis=0, tiled=True), preferr...  34 us
    all_gather x1, waiting for transfers between devices, shards(): full_rows = lax.all_gather(tokens, 'tensor', axis=1, tiled=True)  26.8 us
  transfers between devices with their start and end apart: 7, of which 3 were waited for; matrix products, arithmetic and copies ran while one was open for 11% of the time, Pallas kernels for 0%

commit v1 on v0

v1 whole, which is shorter than its diff:
```python
import jax
import jax.numpy as jnp
from jax import lax
from jax.sharding import PartitionSpec as P

HEADS = 128
HEAD_DIM = 64
GROUPS = 4
STATE = 256
CAP = 2
PCAP = 4
MOST_PAGES = 4

f32 = jnp.float32
bf16 = jnp.bfloat16


def conv_silu(inputs, kernel, request_of):
    floats = inputs.astype(f32)
    total = kernel[3] * floats
    for offset in range(1, 4):
        moved = jnp.concatenate(
            [jnp.zeros((offset, floats.shape[1]), f32), floats[:-offset]], 0
        )
        before = jnp.concatenate([jnp.full((offset,), -1, jnp.int32), request_of[:-offset]], 0)
        total = total + kernel[3 - offset] * jnp.where(
            (before == request_of)[:, None], moved, f32(0.0)
        )
    return jax.nn.silu(total).astype(bf16)


def request_layout(counts, rows_total, page_rows):
    ends = jnp.cumsum(counts)
    page_of = jnp.arange(rows_total, dtype=jnp.int32) // page_rows
    request_of = jnp.sum((page_of[:, None] >= ends[None, :]).astype(jnp.int32), 1)
    last_rows = ends * page_rows - 1
    return (request_of, last_rows, ends)


def ssd_outputs(values, widths, running, keys, queries, request_of):
    scores = jnp.dot(queries, keys.T, preferred_element_type=f32)
    positions = jnp.arange(values.shape[0], dtype=jnp.int32)
    inside = (request_of[:, None] == request_of[None, :]) & (
        positions[None, :] <= positions[:, None]
    )
    gaps = running.T[:, :, None] - running.T[:, None, :]
    decay = jnp.exp(jnp.where(inside[None], gaps, f32(-1e30)))
    mixing = (decay * scores[None]).astype(bf16)
    weighted = (widths[:, :, None] * values).astype(bf16)
    return jnp.einsum("hts,shd->thd", mixing, weighted, preferred_element_type=f32)


def ranks(targets):
    order = jnp.arange(targets.shape[0], dtype=jnp.int32)
    same = targets[None, :] == targets[:, None]
    return jnp.sum((same & (order[None, :] < order[:, None])).astype(jnp.int32), 1)


def slot_items(targets, owner_count, capacity):
    rank = ranks(targets)
    slot = targets * capacity + rank
    slots = jnp.arange(owner_count * capacity, dtype=jnp.int32)
    hit = slot[None, :] == slots[:, None]
    item = jnp.arange(targets.shape[0], dtype=jnp.int32)
    return jnp.sum(jnp.where(hit, item[None, :] + 1, 0), 1) - 1


def pick_rows(rows, table):
    picker = rows[:, None] == jnp.arange(table.shape[0], dtype=jnp.int32)[None, :]
    return jnp.dot(picker.astype(bf16), table, preferred_element_type=f32).astype(bf16)


def slot_of(source, features, count):
    half = count // 2
    swapped = (source % 2 + features) % 2
    return swapped * half + source // 2


def gather_features(scaled):
    dp_count = lax.axis_size("dp")
    tensor_count = lax.axis_size("tensor")
    rows, wide = scaled.shape
    me = lax.axis_index("dp")
    if dp_count == tensor_count and dp_count % 2 == 0:
        perm = []
        for source in range(dp_count):
            for features in range(dp_count):
                perm.append(
                    (
                        source * dp_count + features,
                        features * dp_count + slot_of(source, features, dp_count),
                    )
                )
        moved = lax.ppermute(scaled, ("dp", "tensor"), perm)
        gathered = lax.all_gather(moved, "tensor", axis=0)
        return [
            lax.dynamic_index_in_dim(gathered, slot_of(source, me, dp_count), 0, keepdims=False)
            for source in range(dp_count)
        ]
    full = lax.all_gather(scaled, "tensor", axis=1, tiled=True)
    split = full.reshape(rows, dp_count, -1).transpose(1, 0, 2)
    received = lax.all_to_all(split, "dp", split_axis=0, concat_axis=0, tiled=True)
    return [received[source] for source in range(dp_count)]


def exchange_sums(blocks, weights):
    partial = jnp.stack(
        [jnp.dot(b, weights, preferred_element_type=f32).astype(bf16) for b in blocks]
    )
    received = lax.all_to_all(partial, "dp", split_axis=0, concat_axis=0, tiled=True)
    return jnp.sum(received.astype(f32), 0)


def shards(
    tokens,
    norm_gain,
    w_inner,
    w_groups,
    w_keyval,
    w_step,
    conv_inner,
    conv_groups,
    decay_rate,
    step_bias,
    page_counts,
    owners,
    page_owners,
):
    rows_here, features_here = tokens.shape
    dp_count = lax.axis_size("dp")
    floats = tokens.astype(f32)
    gain = lax.dynamic_slice_in_dim(
        norm_gain, lax.axis_index("tensor") * features_here, features_here, 0
    )
    blocks = gather_features((floats * gain).astype(bf16))
    squares = lax.psum(jnp.sum(floats * floats, -1, keepdims=True), "tensor")
    features = features_here * lax.axis_size("tensor")
    scale = lax.rsqrt(squares / features + 1e-05)

    width_groups = w_groups.shape[1]
    heads_here = decay_rate.shape[0]
    small = jnp.concatenate([w_groups, w_step, w_keyval], 1)
    small_rows = (exchange_sums(blocks, small) * scale).astype(bf16)
    inner_rows = (exchange_sums(blocks, w_inner) * scale).astype(bf16)
    group_rows = small_rows[:, :width_groups]
    step_rows = small_rows[:, width_groups : width_groups + heads_here]
    keyval = small_rows[:, width_groups + heads_here :]

    page_total = page_owners.shape[0]
    page_rows = rows_here // page_total
    in_page = jnp.arange(page_rows, dtype=jnp.int32)
    request_of, last_rows, ends = request_layout(page_counts[0], rows_here, page_rows)

    page_items = slot_items(page_owners[:, 0], dp_count, PCAP)
    page_source = jnp.where(
        page_items[:, None] >= 0, page_items[:, None] * page_rows + in_page[None, :], -1
    )
    page_send = pick_rows(page_source.reshape(-1), keyval).reshape(
        dp_count, PCAP * page_rows, -1
    )

    grouped_local = conv_silu(group_rows, conv_groups, request_of)
    grouped = lax.all_gather(grouped_local, "tensor", axis=1, tiled=True)
    group_id = lax.axis_index("tensor") * heads_here // (HEADS // GROUPS)
    keys = lax.dynamic_slice_in_dim(grouped, group_id * STATE, STATE, 1)
    queries = lax.dynamic_slice_in_dim(grouped, GROUPS * STATE + group_id * STATE, STATE, 1)
    widths = jax.nn.softplus(step_rows.astype(f32) + step_bias)
    running = jnp.cumsum(-decay_rate * widths, 0)
    mixed = conv_silu(inner_rows, conv_inner, request_of)
    values = mixed.astype(f32).reshape(rows_here, heads_here, HEAD_DIM)

    end_running = running[last_rows]
    end_of = jnp.zeros_like(running)
    for r in range(page_counts.shape[1]):
        end_of = jnp.where((request_of == r)[:, None], end_running[r][None, :], end_of)
    reach = jnp.exp(end_of - running) * widths
    reached = (reach[:, :, None] * values).astype(bf16).reshape(rows_here, -1)

    slots = slot_items(owners[:, 0], dp_count, CAP)
    safe = jnp.maximum(slots, 0)
    counts = page_counts[0][safe]
    first = (ends[safe] - counts) * page_rows
    span = jnp.arange(MOST_PAGES * page_rows, dtype=jnp.int32)
    used = (slots[:, None] >= 0) & (span[None, :] < (counts * page_rows)[:, None])
    source = jnp.where(used, first[:, None] + span[None, :], -1).reshape(-1)
    value_send = pick_rows(source, reached).reshape(dp_count, CAP * span.shape[0], -1)
    key_send = pick_rows(source, keys).reshape(dp_count, CAP * span.shape[0], -1)
    tail = jnp.where(
        slots[:, None] >= 0,
        last_rows[safe][:, None] - 2 + jnp.arange(3, dtype=jnp.int32)[None, :],
        -1,
    ).reshape(-1)
    inner_send = pick_rows(tail, inner_rows).reshape(dp_count, CAP * 3, -1)
    group_send = pick_rows(tail, group_rows).reshape(dp_count, CAP * 3, -1)

    def swap(sent):
        return lax.all_to_all(sent, "dp", split_axis=0, concat_axis=0, tiled=True)

    page_received = swap(page_send)
    inner_received = swap(inner_send)
    group_received = swap(group_send)
    value_received = swap(value_send)
    key_received = swap(key_send)

    outputs = ssd_outputs(values, widths, running, keys, queries, request_of)
    ssm_out = outputs.reshape(rows_here, heads_here * HEAD_DIM).astype(bf16)

    slot_count = dp_count * CAP
    states = jnp.einsum(
        "osc,osn->ocn",
        value_received.reshape(slot_count, span.shape[0], -1),
        key_received.reshape(slot_count, span.shape[0], -1),
        preferred_element_type=f32,
    ).astype(bf16)
    return (
        ssm_out,
        states.reshape(slot_count, heads_here, HEAD_DIM, STATE),
        inner_received.reshape(slot_count, 3, -1),
        group_received.reshape(slot_count, 3, -1),
        page_received.reshape(dp_count * PCAP, page_rows, -1),
    )


def solution(mesh):
    in_specs = (
        P(("groups", "dp"), "tensor"),
        P(),
        P("dp", "tensor"),
        P("dp", "tensor"),
        P("dp", "tensor"),
        P("dp", "tensor"),
        P(None, "tensor"),
        P(None, "tensor"),
        P("tensor"),
        P("tensor"),
        P(("groups", "dp"), None),
        P(("groups", "dp"), None),
        P(("groups", "dp"), None),
    )
    out_specs = (
        P(("groups", "dp"), "tensor"),
        P(("groups", "dp"), "tensor", None, None),
        P(("groups", "dp"), None, "tensor"),
        P(("groups", "dp"), None, "tensor"),
        P(("groups", "dp"), None, "tensor"),
    )
    return jax.shard_map(shards, mesh=mesh, in_specs=in_specs, out_specs=out_specs, check_vma=False)
```

time: 1230 us -> 656 us (0.53)
  waiting for transfers between devices: 991 us -> 432 us
  matrix products: 109 us -> 73.5 us
  local copies, waits for them, and re-layouts: 33.9 us -> 46.8 us
  starting transfers between devices: 19.4 us -> 32 us
    all_gather x2 -> x1, waiting for transfers between devices: 854 us -> 147 us  [gather_features(): gathered = lax.all_gather(moved, 'tensor', axis=0)]
    all_to_all x4 -> x7, waiting for transfers between devices: 136 us -> 275 us  [the longest x2 201 us: exchange_sums(): lax.all_to_all(partial, 'dp', split_axis=0, concat_axis=0, tiled=True)]
    dot_general x9 -> x16, matrix products: 109 us -> 73.5 us  [the longest x8 39.9 us: exchange_sums(): jnp.dot(b, weights, preferred_element_type=f32).astype(bf16)]
    all_gather x1 -> x0, blocking collectives: 17.5 us -> none  [shards(): lax.all_gather(w_step, 'dp', axis=0, tiled=True)]
    concatenate x1 -> x0, other arithmetic: 13.2 us -> none  [shards(): joined = jnp.concatenate([w_inner, w_groups, w_keyval], 1)]
    convert_element_type x1 -> x5, other arithmetic: 2.06 us -> 14.8 us  [the longest x1 9.99 us: shards(): values = mixed.astype(f32).reshape(rows_here, heads_here, HEAD_DIM)]
    all_to_all x4 -> x7, starting transfers between devices: 19.3 us -> 31.1 us  [the longest x5 20.4 us: swap(): return lax.all_to_all(sent, 'dp', split_axis=0, concat_axis=0, tiled=True)]
  transfers between devices with their start and end apart: 7 -> 10, of which waited for: 3 -> 7; matrix products, arithmetic and copies ran while one was open for 11% -> 20% of each run, Pallas kernels for 0% -> 0%
where the time goes in v1:
time: 656 us; the launch traced here: 647 us
  waiting for transfers between devices  432 us (66%)
  matrix products  73.5 us (11%)
  local copies, waits for them, and re-layouts  46.8 us (7%)
  other arithmetic  41.3 us (6%)
  starting transfers between devices  32 us (5%)
  between operations  15.3 us (2%)
    all_to_all x2, waiting for transfers between devices, exchange_sums(): lax.all_to_all(partial, 'dp', split_axis=0, concat_axis=0, tiled=True)  201 us
    all_gather x1, waiting for transfers between devices, gather_features(): gathered = lax.all_gather(moved, 'tensor', axis=0)  147 us
    all_to_all x5, waiting for transfers between devices, swap(): return lax.all_to_all(sent, 'dp', split_axis=0, concat_axis=0, tiled=True)  74.8 us
    dot_general x8, matrix products, exchange_sums(): jnp.dot(b, weights, preferred_element_type=f32).astype(bf16)  39.9 us
    all_to_all x5, starting transfers between devices, swap(): return lax.all_to_all(sent, 'dp', split_axis=0, concat_axis=0, tiled=True)  20.4 us
  transfers between devices with their start and end apart: 10, of which 7 were waited for; matrix products, arithmetic and copies ran while one was open for 20% of the time, Pallas kernels for 0%

profile of v1, /device:TPU:0, one launch (start us, length us, event | category | flops | bytes accessed | tf_op | source)
XLA Modules:
  0.0 646.8 jit_solution(17836846962946050123)
XLA Ops:
  7.2 0.7 dynamic_slice.22
  7.9 2.3 fusion.3
  10.2 0.8 collective-permute-start
  11.0 1.3 copy-done.2
  12.7 8.7 %concatenate.37 = bf16[2048,1056]{1,0:T(8,128)(2,1)} concatenate(bf16[2048,512]{1,0:T(8,128)(2,1)} %param.16, bf16[2048,32]{1,0:T(8,128)(2,1)S(1)} %copy.59, bf16[2048,512]{1,0:T(8,128)(2,1)} %param.17), dimensions={1} | concatenate | bytes 8650752 | tf_op jit(solution)/shard_map/concatenate | solution.py:142
  21.4 146.6 %all-gather.6.cloned.1.call-done = bf16[2048,2048]{1,0:T(8,128)(2,1)} async-done(((bf16[512,2048]{1,0:T(8,128)(2,1)}), bf16[2048,2048]{1,0:T(8,128)(2,1)}) %all-gather.6.cloned.1.call-update) | async-done | bytes 8388624 | tf_op jit(solution)/shard_map/all_gather | solution.py:95
  167.9 5.6 fusion.11
  173.5 1.2 copy-done.35
  174.7 2.5 fusion.10
  177.2 2.5 fusion.9
  179.7 2.5 fusion.8
  182.2 2.3 pad_maximum_fusion.1
  184.5 5.1 all-to-all-start
  189.6 8.7 %fusion.7 = bf16[1,512,2048]{2,1,0:T(8,128)(2,1)S(1)} fusion(bf16[2048,2048]{1,0:T(8,128)(2,1)} %param.15, bf16[4,512,2048]{2,1,0:T(8,128)(2,1)} %bitcast.150, s32[]{:T(128)S(6)} %select_n.163), kind=kOutput, calls=%fused_computation.32 | convolution fusion | flops 4296015872 | bytes 12582916 | tf_op jit(solution)/shard_map/dot_general | solution.py:108
  198.3 8.7 %fusion.6 = bf16[1,512,2048]{2,1,0:T(8,128)(2,1)S(1)} fusion(bf16[2048,2048]{1,0:T(8,128)(2,1)} %param.15, bf16[4,512,2048]{2,1,0:T(8,128)(2,1)} %bitcast.151, s32[]{:T(128)S(6)} %select_n.162), kind=kOutput, calls=%fused_computation.31 | convolution fusion | flops 4296015872 | bytes 12582916 | tf_op jit(solution)/shard_map/dot_general | solution.py:108
  207.0 4.8 fusion.5
  211.8 4.8 fusion.4
  216.6 3.9 pad_maximum_fusion
  220.5 65.8 %all-to-all-done = bf16[4,512,1056]{1,2,0:T(8,128)(2,1)} async-done(((bf16[4,512,1056]{1,2,0:T(8,128)(2,1)}), bf16[4,512,1056]{1,2,0:T(8,128)(2,1)}, u32[]{:S(2)}, u32[]{:S(2)}) %all-to-all-start) | async-done | bytes 4325408 | tf_op jit(solution)/shard_map/all_to_all | solution.py:110
  286.3 5.7 all-to-all-start.1
  293.1 1.2 gather_fusion
  294.3 1.2 gather_fusion.1
  295.4 0.6 gather_fusion.3
  296.2 0.7 select_n.189
  296.8 6.2 psum.7
  304.0 0.7 broadcast_compare_fusion.4
  304.7 0.6 fusion.64
  305.3 4.4 convert_reduce_fusion.1
  309.7 2.0 copy.60
  312.5 2.1 multiply_convert_fusion.13
  315.2 1.2 reduce-window.11
  317.5 0.6 exponential_multiply_fusion
  318.2 2.5 mul.271
  320.7 5.5 copy.67
  326.4 0.6 reshape.371
  327.0 1.3 convolution_convert_fusion.11
  328.4 9.5 %all-gather.4.cloned.1.call-done = bf16[512,2048]{1,0:T(8,128)(2,1)} async-done(((bf16[512,512]{1,0:T(8,128)(2,1)}), bf16[512,2048]{1,0:T(8,128)(2,1)}) %all-gather.4.cloned.1.call-update) | async-done | bytes 2097168 | tf_op jit(solution)/shard_map/all_gather | solution.py:163
  337.9 2.3 fusion.32
  340.2 134.8 %all-to-all-done.1 = bf16[4,512,2048]{2,1,0:T(8,128)(2,1)} async-done(((bf16[4,512,2048]{2,1,0:T(8,128)(2,1)}), bf16[4,512,2048]{2,1,0:T(8,128)(2,1)}, u32[]{:S(2)}, u32[]{:S(2)}) %all-to-all-start.1) | async-done | bytes 8388640 | tf_op jit(solution)/shard_map/all_to_all | solution.py:110
  475.0 3.3 all-to-all-start.5
  478.2 7.7 %convert_reduce_fusion = f32[512,2048]{1,0:T(8,128)} fusion(bf16[4,512,2048]{2,1,0:T(8,128)(2,1)} %all-to-all-done.1), kind=kLoop, calls=%fused_computation.5 | loop fusion | flops 7340032 | bytes 12582912 | tf_op jit(solution)/shard_map/reduce_sum | solution.py:111
  485.9 5.1 all-to-all-start.6
  491.0 2.5 multiply_convert_fusion.5
  493.5 2.5 slice.134
  496.0 2.5 slice.133
  498.5 2.4 slice.132
  501.4 0.7 reshape.369
  502.1 2.3 all-to-all-done.6
  504.4 3.7 all-to-all-start.3
  508.2 10.0 %fusion.22 = f32[512,2048]{1,0:T(8,128)} fusion(f32[509,2048]{1,0:T(8,128)} %slice.134, pred[512]{0:T(512)(128)(4,1)S(1)} %copy-done.12, f32[2048]{0:T(1024)S(1)} %bitcast.135, f32[510,2048]{1,0:T(8,128)} %slice.133, pred[512]{0:T(512)(128)(4,1)S(1)} %copy-done.14, f32[2048]{0:T(1024)S(1)} %bitcast.136, f32[511,2048]{1,0:T(8,128)} %slice.132, ...), kind=kLoop, calls=%fused_computation.50 | loop fusion | flops 19922944 | bytes 20958720 | tf_op jit(solution)/shard_map/convert_element_type | solution.py:170
  518.2 3.8 all-to-all-done.3
  522.0 3.3 all-to-all-start.4
  525.3 7.8 %convolution_convert_fusion.1 = bf16[1024,2048]{1,0:T(8,128)(2,1)} fusion(f32[512,2048]{1,0:T(8,128)} %copy.67, f32[512,2048]{1,0:T(8,128)} %fusion.22, s32[1024]{0:T(1024)S(1)} %select_bitcast_fusion), kind=kOutput, calls=%fused_computation.20 | convolution fusion | flops 2152202240 | bytes 12587008 | tf_op jit(solution)/shard_map/dot_general | solution.py:70
  533.1 5.0 all-to-all-start.2
  538.2 0.9 fusion.35
  539.2 0.6 copy.71
  539.9 2.3 fusion.39
  542.2 5.4 copy.62
  547.6 11.2 %fusion.23 = bf16[32,64,512]{2,1,0:T(8,128)(2,1)S(1)} fusion(f32[512,512]{1,0:T(8,128)} %fusion.39, f32[32,512]{1,0:T(8,128)S(1)} %copy-done.4, pred[512,512]{1,0:T(8,128)(4,1)} %fusion.35, f32[512,32,64]{0,2,1:T(8,128)} %bitcast.124, f32[512,32]{0,1:T(8,128)S(1)} %copy.61), kind=kOutput, calls=%fused_computation.51 | convolution fusion | flops 1110441984 | bytes 7733248 | tf_op jit(solution)/shard_map/hts,shd->thd/dot_general | solution.py:50
  558.9 2.4 copy.69
  561.3 0.7 copy.70
  562.0 68.7 %all-to-all-done.2 = bf16[4,256,2048]{2,1,0:T(8,128)(2,1)} async-done(((bf16[4,256,2048]{2,1,0:T(8,128)(2,1)}), bf16[4,256,2048]{2,1,0:T(8,128)(2,1)}, u32[]{:S(2)}, u32[]{:S(2)}) %all-to-all-start.2) | async-done | bytes 4194336 | tf_op jit(solution)/shard_map/all_to_all | solution.py:197
  630.7 8.0 %convolution_convert_fusion = bf16[8,2048,256]{2,1,0:T(8,128)(2,1)} fusion(bf16[8,128,2048]{2,1,0:T(8,128)(2,1)} %bitcast.45, bf16[8,128,256]{2,1,0:T(8,128)(2,1)S(1)} %bitcast.125), kind=kOutput, calls=%fused_computation.10 | convolution fusion | flops 1077936128 | bytes 13107200 | tf_op jit(solution)/shard_map/osc,osn->ocn/dot_general | solution.py:209
  638.7 0.8 copy.76
  (137 shorter events, 5.5 us)
Async XLA Ops:
  7.2 5.2 copy-start.5
  7.2 160.7 %all-gather.6.cloned.1.call-start = ((), (), s32[]{:S(2)}) async-start(), calls=%async_computation.8 | async-start | bytes 10485760 | tf_op jit(solution)/shard_map/all_gather | solution.py:95
  10.2 0.8 collective-permute-start
  11.0 1.3 copy-start.2
  167.9 5.6 copy-start.1
  167.9 6.8 %copy-start.35 = (bf16[2048,2048]{1,0:T(8,128)(2,1)S(1)}, bf16[2048,2048]{1,0:T(8,128)(2,1)}, u32[]{:S(2)}) copy-start(bf16[2048,2048]{1,0:T(8,128)(2,1)} %all-gather.6.cloned.1.call-done) | copy-start | bytes 25165828
  184.5 101.8 %all-to-all-start = ((bf16[4,512,1056]{1,2,0:T(8,128)(2,1)}), bf16[4,512,1056]{1,2,0:T(8,128)(2,1)}, u32[]{:S(2)}, u32[]{:S(2)}) async-start(bf16[4,512,1056]{1,2,0:T(8,128)(2,1)} %pad_maximum_fusion.1), calls=%async_computation | async-start | bytes 8650752 | tf_op jit(solution)/shard_map/all_to_all | solution.py:110
  189.6 17.4 %slice-start = ((s8[8388608]{0:T(1024)(128)(4,1)}), s8[4194304]{0:T(1024)(128)(4,1)S(1)}, s32[]{:S(2)}) async-start(s8[8388608]{0:T(1024)(128)(4,1)} %bitcast.147), calls=%async_computation.9 | async-start | bytes 8388608
  189.6 17.4 %slice-start.2 = ((s8[8388608]{0:T(1024)(128)(4,1)}), s8[4194304]{0:T(1024)(128)(4,1)S(1)}, s32[]{:S(2)}) async-start(s8[8388608]{0:T(1024)(128)(4,1)} %bitcast.155), calls=%async_computation.11 | async-start | bytes 8388608
  198.3 8.7 %slice-start.1 = ((s8[8388608]{0:T(1024)(128)(4,1)}), s8[4194304]{0:T(1024)(128)(4,1)S(1)}, s32[]{:S(2)}) async-start(s8[8388608]{0:T(1024)(128)(4,1)} %bitcast.147), calls=%async_computation.10 | async-start | bytes 8388608
  198.3 8.7 %slice-start.3 = ((s8[8388608]{0:T(1024)(128)(4,1)}), s8[4194304]{0:T(1024)(128)(4,1)S(1)}, s32[]{:S(2)}) async-start(s8[8388608]{0:T(1024)(128)(4,1)} %bitcast.155), calls=%async_computation.12 | async-start | bytes 8388608
  220.4 71.6 %copy-start = (s32[1,8]{1,0:T(1,128)S(1)}, s32[1,8]{1,0:T(1,128)}, u32[]{:S(2)}) copy-start(s32[1,8]{1,0:T(1,128)} %param.23) | copy-start | bytes 100
  220.4 71.8 %copy-start.36 = (f32[32]{0:T(128)S(1)}, f32[32]{0:T(128)}, u32[]{:S(2)}) copy-start(f32[32]{0:T(128)} %param.21) | copy-start | bytes 388
  220.4 72.3 %copy-start.33 = (s32[8,1]{0,1:T(1,128)S(1)}, s32[8,1]{0,1:T(1,128)}, u32[]{:S(2)}) copy-start(s32[8,1]{0,1:T(1,128)} %param.24) | copy-start | bytes 100
  220.4 82.7 %copy-start.34 = (s32[16,1]{0,1:T(1,128)S(1)}, s32[16,1]{0,1:T(1,128)}, u32[]{:S(2)}) copy-start(s32[16,1]{0,1:T(1,128)} %param.25) | copy-start | bytes 196
  220.4 84.3 %copy-start.10 = (f32[4,512]{1,0:T(4,128)S(1)}, f32[4,512]{1,0:T(4,128)}, u32[]{:S(2)}) copy-start(f32[4,512]{1,0:T(4,128)} %param.20) | copy-start | bytes 24580
  286.3 188.7 %all-to-all-start.1 = ((bf16[4,512,2048]{2,1,0:T(8,128)(2,1)}), bf16[4,512,2048]{2,1,0:T(8,128)(2,1)}, u32[]{:S(2)}, u32[]{:S(2)}) async-start(bf16[4,512,2048]{2,1,0:T(8,128)(2,1)} %pad_maximum_fusion), calls=%async_computation.1 | async-start | bytes 16777216 | tf_op jit(solution)/shard_map/all_to_all | solution.py:110
  292.0 45.9 %all-gather.4.cloned.1.call-start = ((), (), s32[]{:S(2)}) async-start(), calls=%async_computation.7 | async-start | bytes 2621440 | tf_op jit(solution)/shard_map/all_gather | solution.py:163
  296.1 9.2 %copy-start.27 = (pred[8]{0:T(512)(128)(4,1)}, pred[8]{0:T(512)(128)(4,1)S(1)}, u32[]{:S(2)}) copy-start(pred[8]{0:T(512)(128)(4,1)S(1)} %add_compare_fusion.2) | copy-start | bytes 28
  303.4 8.3 %copy-start.37 = (s32[16]{0:T(128)}, s32[16]{0:T(128)S(1)}, u32[]{:S(2)}) copy-start(s32[16]{0:T(128)S(1)} %select_reduce_fusion) | copy-start | bytes 196
  311.7 0.7 copy-start.7
  311.8 0.7 copy-start.8
  311.8 0.7 copy-start.9
  311.8 0.7 copy-start.11
  311.8 0.7 copy-start.13
  311.8 0.7 copy-start.15
  312.0 2.5 copy-start.38
  312.0 2.5 copy-start.32
  312.0 2.7 copy-start.29
  312.0 2.7 copy-start.30
  312.1 2.7 copy-start.28
  312.1 2.8 copy-start.6
  312.1 2.8 copy-start.17
  312.1 2.8 copy-start.31
  312.1 5.3 copy-start.19
  312.1 5.3 copy-start.20
  312.1 5.3 copy-start.21
  312.1 5.3 copy-start.22
  312.1 5.3 copy-start.23
  312.1 5.3 copy-start.24
  312.2 5.3 copy-start.25
  312.2 5.3 copy-start.26
  316.7 0.7 copy-start.3
  320.7 5.5 copy-start.18
  475.0 11.0 %all-to-all-start.5 = ((bf16[4,6,512]{2,1,0:T(8,128)(2,1)}), bf16[4,6,512]{2,1,0:T(8,128)(2,1)S(1)}, u32[]{:S(2)}, u32[]{:S(2)}) async-start(bf16[4,6,512]{2,1,0:T(8,128)(2,1)} %reshape.371), calls=%async_computation.5 | async-start | bytes 65536 | tf_op jit(solution)/shard_map/all_to_all | solution.py:197
  485.9 18.5 %all-to-all-start.6 = ((bf16[4,128,512]{2,1,0:T(8,128)(2,1)}), bf16[4,128,512]{2,1,0:T(8,128)(2,1)S(1)}, u32[]{:S(2)}, u32[]{:S(2)}) async-start(bf16[4,128,512]{2,1,0:T(8,128)(2,1)} %bitcast.50), calls=%async_computation.6 | async-start | bytes 1048576 | tf_op jit(solution)/shard_map/all_to_all | solution.py:197
  498.5 9.6 %copy-start.12 = (pred[512]{0:T(512)(128)(4,1)S(1)}, pred[512]{0:T(512)(128)(4,1)}, u32[]{:S(2)}) copy-start(pred[512]{0:T(512)(128)(4,1)} %get-tuple-element.58) | copy-start | bytes 1540
  498.5 9.6 %copy-start.14 = (pred[512]{0:T(512)(128)(4,1)S(1)}, pred[512]{0:T(512)(128)(4,1)}, u32[]{:S(2)}) copy-start(pred[512]{0:T(512)(128)(4,1)} %get-tuple-element.59) | copy-start | bytes 1540
  498.5 9.6 %copy-start.16 = (pred[512]{0:T(512)(128)(4,1)S(1)}, pred[512]{0:T(512)(128)(4,1)}, u32[]{:S(2)}) copy-start(pred[512]{0:T(512)(128)(4,1)} %get-tuple-element.60) | copy-start | bytes 1540
  504.4 17.6 %all-to-all-start.3 = ((bf16[4,256,256]{2,1,0:T(8,128)(2,1)}), bf16[4,256,256]{2,1,0:T(8,128)(2,1)S(1)}, u32[]{:S(2)}, u32[]{:S(2)}) async-start(bf16[4,256,256]{2,1,0:T(8,128)(2,1)} %bitcast.46), calls=%async_computation.3 | async-start | bytes 1048576 | tf_op jit(solution)/shard_map/all_to_all | solution.py:197
  522.0 11.2 %all-to-all-start.4 = ((bf16[4,6,2048]{2,1,0:T(8,128)(2,1)}), bf16[4,6,2048]{2,1,0:T(8,128)(2,1)S(1)}, u32[]{:S(2)}, u32[]{:S(2)}) async-start(bf16[4,6,2048]{2,1,0:T(8,128)(2,1)} %reshape.369), calls=%async_computation.4 | async-start | bytes 262144 | tf_op jit(solution)/shard_map/all_to_all | solution.py:197
  533.1 97.6 %all-to-all-start.2 = ((bf16[4,256,2048]{2,1,0:T(8,128)(2,1)}), bf16[4,256,2048]{2,1,0:T(8,128)(2,1)}, u32[]{:S(2)}, u32[]{:S(2)}) async-start(bf16[4,256,2048]{2,1,0:T(8,128)(2,1)} %bitcast.123), calls=%async_computation.2 | async-start | bytes 8388608 | tf_op jit(solution)/shard_map/all_to_all | solution.py:197
  542.2 5.4 copy-start.4
Sparse Core Ops, SparseCore 0:
  12.5 155.3 all-gather.5
  314.7 23.1 all-gather.3

commit v2 on v1

--- a/solution.py
+++ b/solution.py
@@ -1,6 +1,10 @@
+import functools
+
 import jax
 import jax.numpy as jnp
 from jax import lax
+from jax.experimental import pallas as pl
+from jax.experimental.pallas import tpu as pltpu
 from jax.sharding import PartitionSpec as P
 
 HEADS = 128
@@ -76,27 +80,275 @@
     return swapped * half + source // 2
 
 
+PIECES = 4
+CHUNK = 640
+MESH = pl.DeviceIdType.MESH
+VMEM_LIMIT = 58 * 2**20
+
+
+def share_kernel(count, x_ref, out_ref, send_sem, recv_sem):
+    group = lax.axis_index("groups")
+    dp = lax.axis_index("dp")
+    ten = lax.axis_index("tensor")
+    half = count // 2
+    rows = x_ref.shape[0] // PIECES
+
+    def source_at(slot):
+        return lax.rem(slot, half) * 2 + lax.rem(slot // half + dp, 2)
+
+    target = slot_of(dp, ten, count)
+    mine = source_at(ten)
+    sibling = ten + 1 - 2 * lax.rem(ten, 2)
+    across = lax.rem(ten + half, count)
+    beyond = lax.rem(sibling + half, count)
+    stays = (ten == dp) & (target == ten)
+
+    barrier = pltpu.get_barrier_semaphore()
+
+    @pl.when(jnp.logical_not(stays))
+    def _():
+        pl.semaphore_signal(barrier, inc=1, device_id=(group, mine, dp), device_id_type=MESH)
+
+    for peer in (sibling, across):
+        pl.semaphore_signal(barrier, inc=1, device_id=(group, dp, peer), device_id_type=MESH)
+
+    @pl.when(jnp.logical_not(stays))
+    def _():
+        pl.semaphore_wait(barrier, 3)
+
+    @pl.when(stays)
+    def _():
+        pl.semaphore_wait(barrier, 2)
+
+    def move(source, block, piece, kind, device):
+        part = pl.ds(piece * rows, rows)
+        return pltpu.make_async_remote_copy(
+            src_ref=x_ref.at[part] if source is None else out_ref.at[source, part],
+            dst_ref=out_ref.at[block, part],
+            send_sem=send_sem.at[kind, piece],
+            recv_sem=recv_sem.at[kind, piece],
+            device_id=device,
+            device_id_type=MESH,
+        )
+
+    def local(piece):
+        part = pl.ds(piece * rows, rows)
+        return pltpu.make_async_copy(x_ref.at[part], out_ref.at[dp, part], send_sem.at[0, piece])
+
+    to_target = (group, ten, target)
+    to_sibling = (group, dp, sibling)
+    to_across = (group, dp, across)
+
+    @pl.when(stays)
+    def _():
+        for piece in range(PIECES):
+            local(piece).start()
+
+    @pl.when(jnp.logical_not(stays))
+    def _():
+        for piece in range(PIECES):
+            move(None, dp, piece, 0, to_target).start()
+
+    for piece in range(PIECES):
+
+        @pl.when(stays)
+        def _():
+            local(piece).wait()
+
+        @pl.when(jnp.logical_not(stays))
+        def _():
+            move(None, mine, piece, 0, to_target).wait_recv()
+
+        move(mine, mine, piece, 2, to_across).start()
+        move(mine, mine, piece, 1, to_sibling).start()
+    far = source_at(across)
+    for piece in range(PIECES):
+        move(far, far, piece, 2, to_across).wait_recv()
+        move(far, far, piece, 3, to_sibling).start()
+    near = source_at(sibling)
+    last = source_at(beyond)
+    for piece in range(PIECES):
+        move(near, near, piece, 1, to_sibling).wait_recv()
+        move(last, last, piece, 3, to_sibling).wait_recv()
+
+    @pl.when(jnp.logical_not(stays))
+    def _():
+        for piece in range(PIECES):
+            move(None, dp, piece, 0, to_target).wait_send()
+
+    for piece in range(PIECES):
+        move(mine, mine, piece, 2, to_across).wait_send()
+        move(mine, mine, piece, 1, to_sibling).wait_send()
+        move(far, far, piece, 3, to_sibling).wait_send()
+
+
+def share_blocks(scaled):
+    count = lax.axis_size("dp")
+    return pl.pallas_call(
+        functools.partial(share_kernel, count),
+        out_shape=jax.ShapeDtypeStruct((count,) + scaled.shape, bf16),
+        in_specs=[pl.BlockSpec(memory_space=pl.ANY)],
+        out_specs=pl.BlockSpec(memory_space=pl.ANY),
+        scratch_shapes=[
+            pltpu.SemaphoreType.DMA((4, PIECES)),
+            pltpu.SemaphoreType.DMA((4, PIECES)),
+        ],
+        compiler_params=pltpu.CompilerParams(collective_id=0, has_side_effects=True),
+    )(scaled)
+
+
+def line_kernel(
+    count, widths, x_hbm, *refs
+):
+    weights = refs[: len(widths)]
+    out_ref, x_ref, w_ref, held, part, load_sem, send_sem, recv_sem = refs[len(widths) :]
+    group = lax.axis_index("groups")
+    dp = lax.axis_index("dp")
+    ten = lax.axis_index("tensor")
+    chunks = w_ref.shape[1] // CHUNK
+
+    loads = [pltpu.make_async_copy(x_hbm, x_ref, load_sem.at[0])]
+    start = 0
+    for index, width in enumerate(widths):
+        loads.append(
+            pltpu.make_async_copy(
+                weights[index], w_ref.at[:, pl.ds(start, width)], load_sem.at[index + 1]
+            )
+        )
+        start += width
+    for load in loads:
+        load.start()
+
+    barrier = pltpu.get_barrier_semaphore()
+    right = (group, dp + 1, ten)
+    left = (group, dp - 1, ten)
+    has_left = dp > 0
+    has_right = dp < count - 1
+
+    @pl.when(has_left)
+    def _():
+        pl.semaphore_signal(barrier, inc=1, device_id=left, device_id_type=MESH)
+
+    @pl.when(has_right)
+    def _():
+        pl.semaphore_signal(barrier, inc=1, device_id=right, device_id_type=MESH)
+
+    @pl.when(has_left & has_right)
+    def _():
+        pl.semaphore_wait(barrier, 2)
+
+    @pl.when(jnp.logical_not(has_left & has_right))
+    def _():
+        pl.semaphore_wait(barrier, 1)
+
+    for load in loads:
+        load.wait()
+
+    def move(slot, chunk, device):
+        return pltpu.make_async_remote_copy(
+            src_ref=held.at[slot, chunk],
+            dst_ref=held.at[slot, chunk],
+            send_sem=send_sem.at[slot, chunk],
+            recv_sem=recv_sem.at[slot, chunk],
+            device_id=device,
+            device_id_type=MESH,
+        )
+
+    def project(block, chunk):
+        columns = pl.ds(pl.multiple_of(chunk * CHUNK, 128), CHUNK)
+        part[...] = jnp.dot(x_ref[block], w_ref[:, columns], preferred_element_type=f32)
+
+    def step(block, slot, chunk, has_source, device):
+        project(block, chunk)
+
+        @pl.when(has_source)
+        def _():
+            move(slot, chunk, device).wait_recv()
+            held[slot, chunk] = (part[...] + held[slot, chunk].astype(f32)).astype(bf16)
+
+        @pl.when(jnp.logical_not(has_source))
+        def _():
+            held[slot, chunk] = part[...].astype(bf16)
+
+        move(slot, chunk, device).start()
+
+    @pl.loop(0, chunks)
+    def _(chunk):
+        @pl.loop(0, count - 1 - dp)
+        def _(back):
+            block = count - 1 - back
+            step(block, block + 1, chunk, has_left, right)
+
+        @pl.loop(0, dp)
+        def _(block):
+            step(block, block, chunk, has_right, left)
+
+    @pl.loop(0, chunks)
+    def _(chunk):
+        columns = pl.ds(pl.multiple_of(chunk * CHUNK, 128), CHUNK)
+        project(dp, chunk)
+
+        @pl.when(has_left)
+        def _():
+            move(dp + 1, chunk, left).wait_recv()
+            part[...] += held[dp + 1, chunk].astype(f32)
+
+        @pl.when(has_right)
+        def _():
+            move(dp, chunk, right).wait_recv()
+            part[...] += held[dp, chunk].astype(f32)
+
+        out_ref[:, columns] = part[...]
+
+    @pl.loop(0, chunks)
+    def _(chunk):
+        @pl.loop(0, count - 1 - dp)
+        def _(back):
+            move(count - back, chunk, right).wait_send()
+
+        @pl.loop(0, dp)
+        def _(block):
+            move(block, chunk, left).wait_send()
+
+
+def line_sums(blocks, weights):
+    count, rows, depth = blocks.shape
+    widths = [w.shape[1] for w in weights]
+    total = sum(widths)
+    chunks = total // CHUNK
+    return pl.pallas_call(
+        functools.partial(line_kernel, count, widths),
+        out_shape=jax.ShapeDtypeStruct((rows, total), f32),
+        in_specs=[pl.BlockSpec(memory_space=pl.ANY)] * (1 + len(weights)),
+        out_specs=pl.BlockSpec(memory_space=pltpu.VMEM),
+        scratch_shapes=[
+            pltpu.VMEM((count, rows, depth), bf16),
+            pltpu.VMEM((depth, total), bf16),
+            pltpu.VMEM((count + 1, chunks, rows, CHUNK), bf16),
+            pltpu.VMEM((rows, CHUNK), f32),
+            pltpu.SemaphoreType.DMA((1 + len(weights),)),
+            pltpu.SemaphoreType.DMA((count + 1, chunks)),
+            pltpu.SemaphoreType.DMA((count + 1, chunks)),
+        ],
+        compiler_params=pltpu.CompilerParams(
+            collective_id=1, has_side_effects=True, vmem_limit_bytes=VMEM_LIMIT
+        ),
+        cost_estimate=pl.CostEstimate(
+            flops=2 * count * rows * depth * total,
+            bytes_accessed=2 * (depth * total + count * rows * depth),
+            transcendentals=0,
+        ),
+    )(blocks, *weights)
+
+
+def pad_columns(weights, multiple):
+    extra = -weights.shape[1] % multiple
+    return jnp.pad(weights, ((0, 0), (0, extra)))
+
+
 def gather_features(scaled):
     dp_count = lax.axis_size("dp")
-    tensor_count = lax.axis_size("tensor")
-    rows, wide = scaled.shape
-    me = lax.axis_index("dp")
-    if dp_count == tensor_count and dp_count % 2 == 0:
-        perm = []
-        for source in range(dp_count):
-            for features in range(dp_count):
-                perm.append(
-                    (
-                        source * dp_count + features,
-                        features * dp_count + slot_of(source, features, dp_count),
-                    )
-                )
-        moved = lax.ppermute(scaled, ("dp", "tensor"), perm)
-        gathered = lax.all_gather(moved, "tensor", axis=0)
-        return [
-            lax.dynamic_index_in_dim(gathered, slot_of(source, me, dp_count), 0, keepdims=False)
-            for source in range(dp_count)
-        ]
+    rows = scaled.shape[0]
     full = lax.all_gather(scaled, "tensor", axis=1, tiled=True)
     split = full.reshape(rows, dp_count, -1).transpose(1, 0, 2)
     received = lax.all_to_all(split, "dp", split_axis=0, concat_axis=0, tiled=True)
@@ -132,19 +384,26 @@
     gain = lax.dynamic_slice_in_dim(
         norm_gain, lax.axis_index("tensor") * features_here, features_here, 0
     )
-    blocks = gather_features((floats * gain).astype(bf16))
+    scaled = (floats * gain).astype(bf16)
     squares = lax.psum(jnp.sum(floats * floats, -1, keepdims=True), "tensor")
     features = features_here * lax.axis_size("tensor")
     scale = lax.rsqrt(squares / features + 1e-05)
 
     width_groups = w_groups.shape[1]
     heads_here = decay_rate.shape[0]
-    small = jnp.concatenate([w_groups, w_step, w_keyval], 1)
-    small_rows = (exchange_sums(blocks, small) * scale).astype(bf16)
-    inner_rows = (exchange_sums(blocks, w_inner) * scale).astype(bf16)
-    group_rows = small_rows[:, :width_groups]
-    step_rows = small_rows[:, width_groups : width_groups + heads_here]
-    keyval = small_rows[:, width_groups + heads_here :]
+    width_keyval = w_keyval.shape[1]
+    pieces = [w_groups, w_keyval, pad_columns(w_step, 128), w_inner]
+    total = sum(piece.shape[1] for piece in pieces)
+    if dp_count == lax.axis_size("tensor") and dp_count == 4 and total % CHUNK == 0:
+        sums = line_sums(share_blocks(scaled), pieces) * scale
+    else:
+        blocks = gather_features(scaled)
+        sums = exchange_sums(blocks, jnp.concatenate(pieces, 1)) * scale
+    group_rows = sums[:, :width_groups].astype(bf16)
+    keyval = sums[:, width_groups : width_groups + width_keyval].astype(bf16)
+    first_step = width_groups + width_keyval
+    step_rows = sums[:, first_step : first_step + heads_here].astype(bf16)
+    inner_rows = sums[:, total - w_inner.shape[1] :].astype(bf16)
 
     page_total = page_owners.shape[0]
     page_rows = rows_here // page_total

time: 656 us -> 571 us (0.87); the launches traced: 647 us -> 569 us
  waiting for transfers between devices: 432 us -> 84.1 us
  Pallas kernels: 0 us -> 345 us
  matrix products: 73.5 us -> 33 us
  local copies, waits for them, and re-layouts: 46.8 us -> 32.2 us
  other arithmetic: 41.3 us -> 30.7 us
  starting transfers between devices: 32 us -> 22.3 us
    pallas_call x0 -> x2, Pallas kernels: none -> 345 us  [the longest x1 245 us: line_sums(): pl.pallas_call(functools.partial(line_kernel, count, widths), out_shape=j...]
    all_to_all x2 -> x0, waiting for transfers between devices: 201 us -> none  [exchange_sums(): lax.all_to_all(partial, 'dp', split_axis=0, concat_axis=0, tiled=True)]
    all_gather x1 -> x0, waiting for transfers between devices: 147 us -> none  [gather_features(): gathered = lax.all_gather(moved, 'tensor', axis=0)]
    dot_general x8 -> x0, matrix products: 39.9 us -> none  [exchange_sums(): jnp.dot(b, weights, preferred_element_type=f32).astype(bf16)]
    reduce_sum x2 -> x0, other arithmetic: 12.1 us -> none  [exchange_sums(): return jnp.sum(received.astype(f32), 0)]
    all_to_all x2 -> x0, starting transfers between devices: 10.7 us -> none  [exchange_sums(): lax.all_to_all(partial, 'dp', split_axis=0, concat_axis=0, tiled=True)]
    all_gather x1, waiting for transfers between devices: 9.52 us -> 0.01 us  [shards(): grouped = lax.all_gather(grouped_local, 'tensor', axis=1, tiled=True)]
    all_to_all x5, waiting for transfers between devices: 74.8 us -> 84.1 us  [swap(): return lax.all_to_all(sent, 'dp', split_axis=0, concat_axis=0, tiled=True)]
  transfers between devices with their start and end apart: 10 -> 6, of which waited for: 7 -> 3; matrix products, arithmetic and copies ran while one was open for 20% -> 13% of each run, Pallas kernels for 0% -> 0%
where the time goes in v2:
time: 571 us; the launch traced here: 569 us
  Pallas kernels  345 us (60%)
  waiting for transfers between devices  84.1 us (15%)
  matrix products  33 us (6%)
  local copies, waits for them, and re-layouts  32.2 us (6%)
  other arithmetic  30.7 us (5%)
  starting transfers between devices  22.3 us (4%)
  between operations  14.3 us (3%)
  blocking collectives  8.31 us (1%)
    pallas_call x1, Pallas kernels, line_sums(): pl.pallas_call(functools.partial(line_kernel, count, widths), out_shape=j...  245 us
    pallas_call x1, Pallas kernels, share_blocks(): pl.pallas_call(functools.partial(share_kernel, count), out_shape=jax.Shap...  99.1 us
    all_to_all x5, waiting for transfers between devices, swap(): return lax.all_to_all(sent, 'dp', split_axis=0, concat_axis=0, tiled=True)  84.1 us
    all_to_all x5, starting transfers between devices, swap(): return lax.all_to_all(sent, 'dp', split_axis=0, concat_axis=0, tiled=True)  22.1 us
    dot_general x5, matrix products, pick_rows(): jnp.dot(picker.astype(bf16), table, preferred_element_type=f32).astype(bf16)  12.6 us
  transfers between devices with their start and end apart: 6, of which 3 were waited for; matrix products, arithmetic and copies ran while one was open for 13% of the time, Pallas kernels for 0%

profile of v2, /device:TPU:0, one launch (start us, length us, event | category | flops | bytes accessed | tf_op | source)
XLA Modules:
  0.0 569.4 jit_solution(5178457033588930312)
XLA Ops:
  7.2 0.9 convert_reduce_fusion.2
  8.1 0.7 iota_add_fusion.1
  8.9 0.8 reduce-window.10
  9.7 0.6 gather_fusion.3
  10.5 1.2 copy.39
  11.7 0.7 dynamic_slice.9
  12.4 3.5 fusion.3
  16.0 8.3 %psum.7 = f32[512,1]{0,1:T(1,128)S(1)} all-reduce(f32[512,1]{0,1:T(1,128)S(1)} %bitcast.99), channel_id=1, replica_groups=mesh['groups'=2,'dp'=4,'tensor'=4] {'tensor'}, use_global_device_ids=true, to_apply=%region_1.0 | all-reduce | flops 512 | bytes 4096 | tf_op jit(solution)/shard_map/psum | solution.py:388
  24.3 99.1 %shard_map.164.x_hbm = bf16[4,512,2048]{2,1,0:T(8,128)(2,1)} custom-call(bf16[512,2048]{1,0:T(8,128)(2,1)} %get-tuple-element.23.x_ref), custom_call_target="tpu_custom_call" | custom-call | tf_op jit(solution)/shard_map/pallas_call | solution.py:187
  123.4 0.9 pad.12.refs_2_
  124.3 245.5 %shard_map.165 = f32[512,3200]{1,0:T(8,128)} custom-call(bf16[4,512,2048]{2,1,0:T(8,128)(2,1)} %shard_map.164.x_hbm, bf16[2048,512]{1,0:T(8,128)(2,1)} %refs_0_.1, bf16[2048,512]{1,0:T(8,128)(2,1)} %refs_1_.1, bf16[2048,128]{1,0:T(8,128)(2,1)} %pad.12.refs_2_, bf16[2048,2048]{1,0:T(8,128)(2,1)} %refs_3_.1), custom_call_target="tpu_custom_call" | custom-call | flops 26843545600 | bytes 21495808 | tf_op jit(solution)/shard_map/pallas_call | solution.py:319
  369.7 3.5 multiply_convert_fusion.2
  373.3 0.2 convolution_convert_fusion.4
  373.5 0.6 reshape.371
  374.1 3.9 all-to-all-start.3
  378.0 0.2 all-gather.2.cloned.1.call-start
  378.5 0.6 broadcast_compare_fusion.4
  379.1 2.1 multiply_convert_fusion.12
  381.2 0.2 convert_reduce_fusion.1
  381.6 1.1 convolution_convert_fusion.2
  382.6 0.5 neg.17
  383.3 1.3 convolution_convert_fusion.3
  384.6 1.5 compare_select_fusion
  386.1 0.7 copy.42
  386.9 2.3 reduce-window.11
  389.2 0.2 slice_reduce_fusion
  389.4 0.7 broadcast_add_fusion
  390.1 0.6 gather_fusion.1
  390.7 0.6 gather_fusion
  391.4 0.9 fusion.32
  392.3 0.5 slice_convert_fusion
  392.9 7.2 %fusion.6 = f32[512,2048]{1,0:T(8,128)} fusion(f32[509,2048]{1,0:T(8,128)S(1)} %bitcast.72, pred[512]{0:T(512)(128)(4,1)} %copy-done.4, f32[2048]{0:T(1024)S(1)} %bitcast.93, f32[510,2048]{1,0:T(8,128)S(1)} %bitcast.73, pred[512]{0:T(512)(128)(4,1)} %copy-done.5, f32[2048]{0:T(1024)S(1)} %bitcast.94, f32[511,2048]{1,0:T(8,128)S(1)} %bitcast.74, ...), kind=kLoop, calls=%fused_computation.21 | loop fusion | flops 17825792 | bytes 18859520 | tf_op jit(solution)/shard_map/convert_element_type | solution.py:429
  400.0 0.5 broadcast_multiply_fusion.1
  400.6 0.7 reshape.369
  401.3 1.0 copy.43
  402.3 4.8 all-to-all-start.2
  407.1 0.5 fusion.28
  407.6 6.1 %all-to-all-done.2 = bf16[4,6,2048]{2,1,0:T(8,128)(2,1)} async-done(((bf16[4,6,2048]{2,1,0:T(8,128)(2,1)}), bf16[4,6,2048]{2,1,0:T(8,128)(2,1)}, u32[]{:S(2)}, u32[]{:S(2)}) %all-to-all-start.2) | async-done | bytes 98336 | tf_op jit(solution)/shard_map/all_to_all | solution.py:456
  413.7 4.1 all-to-all-start.4
  417.8 0.7 pad_clamp_fusion
  418.5 0.6 gather_fusion.2
  419.1 0.8 select_bitcast_fusion
  419.8 0.6 slice_bitcast_fusion.7
  420.4 2.3 fusion.9
  422.7 9.0 %all-to-all-done.4 = bf16[4,128,512]{2,1,0:T(8,128)(2,1)} async-done(((bf16[4,128,512]{2,1,0:T(8,128)(2,1)}), bf16[4,128,512]{2,1,0:T(8,128)(2,1)}, u32[]{:S(2)}, u32[]{:S(2)}) %all-to-all-start.4) | async-done | bytes 524320 | tf_op jit(solution)/shard_map/all_to_all | solution.py:456
  431.7 4.1 all-to-all-start.1
  435.8 2.3 exponential_multiply_fusion
  438.1 1.1 copy.46
  439.2 2.5 mul.251
  441.7 5.4 copy.47
  447.1 7.8 %convolution_convert_fusion.1 = bf16[1024,2048]{1,0:T(8,128)(2,1)} fusion(f32[512,2048]{1,0:T(8,128)} %copy.47, f32[512,2048]{1,0:T(8,128)} %fusion.6, s32[1024]{0:T(1024)S(1)} %select_bitcast_fusion), kind=kOutput, calls=%fused_computation.16 | convolution fusion | flops 2152202240 | bytes 12587008 | tf_op jit(solution)/shard_map/dot_general | solution.py:74
  454.9 5.1 all-to-all-start
  460.0 5.4 copy.41
  465.6 0.2 fusion.12
  465.8 0.8 reshape.372
  466.6 0.6 copy.51
  467.2 1.0 reshape.370
  468.2 0.7 copy.50
  468.9 1.4 fusion.16
  470.3 11.0 %fusion.7 = bf16[32,64,512]{2,1,0:T(8,128)(2,1)S(1)} fusion(f32[512,512]{1,0:T(8,128)S(1)} %fusion.16, f32[32,512]{1,0:T(8,128)S(1)} %copy.44, pred[512,512]{1,0:T(8,128)(4,1)S(1)} %fusion.12, f32[512,32,64]{0,2,1:T(8,128)} %bitcast.81, f32[512,32]{0,1:T(8,128)S(1)} %copy.40), kind=kOutput, calls=%fused_computation.22 | convolution fusion | flops 1110441984 | bytes 7733248 | tf_op jit(solution)/shard_map/hts,shd->thd/dot_general | solution.py:54
  481.2 2.4 copy.49
  483.6 69.0 %all-to-all-done = bf16[4,256,2048]{2,1,0:T(8,128)(2,1)} async-done(((bf16[4,256,2048]{2,1,0:T(8,128)(2,1)}), bf16[4,256,2048]{2,1,0:T(8,128)(2,1)}, u32[]{:S(2)}, u32[]{:S(2)}) %all-to-all-start) | async-done | bytes 4194336 | tf_op jit(solution)/shard_map/all_to_all | solution.py:456
  552.6 8.1 %convolution_convert_fusion = bf16[8,2048,256]{2,1,0:T(8,128)(2,1)} fusion(bf16[8,128,2048]{2,1,0:T(8,128)(2,1)} %bitcast.33, bf16[8,128,256]{2,1,0:T(8,128)(2,1)} %bitcast.35), kind=kOutput, calls=%fused_computation.8 | convolution fusion | flops 1077936128 | bytes 13107200 | tf_op jit(solution)/shard_map/osc,osn->ocn/dot_general | solution.py:468
  560.7 1.9 copy.54
  (49 shorter events, 1.1 us)
Async XLA Ops:
  8.9 7.1 %copy-start.8 = (pred[8]{0:T(512)(128)(4,1)}, pred[8]{0:T(512)(128)(4,1)S(1)}, u32[]{:S(2)}) copy-start(pred[8]{0:T(512)(128)(4,1)S(1)} %add_compare_fusion.2) | copy-start | bytes 28
  369.7 8.6 %copy-start.3 = (f32[4,512]{1,0:T(4,128)S(1)}, f32[4,512]{1,0:T(4,128)}, u32[]{:S(2)}) copy-start(f32[4,512]{1,0:T(4,128)} %param.20) | copy-start | bytes 24580
  373.2 8.0 %copy-start.9 = (s32[16,1]{0,1:T(1,128)S(1)}, s32[16,1]{0,1:T(1,128)}, u32[]{:S(2)}) copy-start(s32[16,1]{0,1:T(1,128)} %param.25) | copy-start | bytes 196
  374.1 28.1 %all-to-all-start.3 = ((bf16[4,6,512]{2,1,0:T(8,128)(2,1)}), bf16[4,6,512]{2,1,0:T(8,128)(2,1)}, u32[]{:S(2)}, u32[]{:S(2)}) async-start(bf16[4,6,512]{2,1,0:T(8,128)(2,1)} %reshape.371), calls=%async_computation.3 | async-start | bytes 65536 | tf_op jit(solution)/shard_map/all_to_all | solution.py:456
  378.0 42.4 %all-gather.2.cloned.1.call-start = ((), (), s32[]{:S(2)}) async-start(), calls=%async_computation.5 | async-start | bytes 2621440 | tf_op jit(solution)/shard_map/all_gather | solution.py:422
  378.2 4.4 copy-start.10
  379.1 4.2 copy-start.4
  379.1 4.2 copy-start.5
  379.1 4.2 copy-start.6
  379.1 11.6 %copy-start = (s32[1,8]{1,0:T(1,128)S(1)}, s32[1,8]{1,0:T(1,128)}, u32[]{:S(2)}) copy-start(s32[1,8]{1,0:T(1,128)} %param.23) | copy-start | bytes 100
  392.9 7.7 %copy-start.2 = (bf16[24,2048]{1,0:T(8,128)(2,1)S(1)}, bf16[24,2048]{1,0:T(8,128)(2,1)}, u32[]{:S(2)}) copy-start(bf16[24,2048]{1,0:T(8,128)(2,1)} %convolution_convert_fusion.2) | copy-start | bytes 294916
  400.0 35.8 %copy-start.7 = (f32[32]{0:T(128)S(1)}, f32[32]{0:T(128)}, u32[]{:S(2)}) copy-start(f32[32]{0:T(128)} %param.22) | copy-start | bytes 388
  402.3 11.4 %all-to-all-start.2 = ((bf16[4,6,2048]{2,1,0:T(8,128)(2,1)}), bf16[4,6,2048]{2,1,0:T(8,128)(2,1)}, u32[]{:S(2)}, u32[]{:S(2)}) async-start(bf16[4,6,2048]{2,1,0:T(8,128)(2,1)} %reshape.369), calls=%async_computation.2 | async-start | bytes 262144 | tf_op jit(solution)/shard_map/all_to_all | solution.py:456
  413.7 18.0 %all-to-all-start.4 = ((bf16[4,128,512]{2,1,0:T(8,128)(2,1)}), bf16[4,128,512]{2,1,0:T(8,128)(2,1)}, u32[]{:S(2)}, u32[]{:S(2)}) async-start(bf16[4,128,512]{2,1,0:T(8,128)(2,1)} %bitcast.86), calls=%async_computation.4 | async-start | bytes 1048576 | tf_op jit(solution)/shard_map/all_to_all | solution.py:456
  431.7 23.2 %all-to-all-start.1 = ((bf16[4,256,256]{2,1,0:T(8,128)(2,1)}), bf16[4,256,256]{2,1,0:T(8,128)(2,1)}, u32[]{:S(2)}, u32[]{:S(2)}) async-start(bf16[4,256,256]{2,1,0:T(8,128)(2,1)} %bitcast.87), calls=%async_computation.1 | async-start | bytes 1048576 | tf_op jit(solution)/shard_map/all_to_all | solution.py:456
  454.9 97.7 %all-to-all-start = ((bf16[4,256,2048]{2,1,0:T(8,128)(2,1)}), bf16[4,256,2048]{2,1,0:T(8,128)(2,1)}, u32[]{:S(2)}, u32[]{:S(2)}) async-start(bf16[4,256,2048]{2,1,0:T(8,128)(2,1)} %bitcast.80), calls=%async_computation | async-start | bytes 8388608 | tf_op jit(solution)/shard_map/all_to_all | solution.py:456
  460.0 5.4 copy-start.1
Sparse Core Ops, SparseCore 0:
  381.3 25.6 all-gather.1

commit v3 on v2

--- a/solution.py
+++ b/solution.py
@@ -41,17 +41,23 @@
     return (request_of, last_rows, ends)
 
 
-def ssd_outputs(values, widths, running, keys, queries, request_of):
+def ssd_outputs(weighted, running, keys, queries, request_of):
     scores = jnp.dot(queries, keys.T, preferred_element_type=f32)
-    positions = jnp.arange(values.shape[0], dtype=jnp.int32)
+    positions = jnp.arange(weighted.shape[0], dtype=jnp.int32)
     inside = (request_of[:, None] == request_of[None, :]) & (
         positions[None, :] <= positions[:, None]
     )
     gaps = running.T[:, :, None] - running.T[:, None, :]
     decay = jnp.exp(jnp.where(inside[None], gaps, f32(-1e30)))
     mixing = (decay * scores[None]).astype(bf16)
-    weighted = (widths[:, :, None] * values).astype(bf16)
     return jnp.einsum("hts,shd->thd", mixing, weighted, preferred_element_type=f32)
+
+
+def spread(per_head):
+    heads = per_head.shape[1]
+    channel = jnp.arange(heads * HEAD_DIM, dtype=jnp.int32) // HEAD_DIM
+    table = (channel[None, :] == jnp.arange(heads, dtype=jnp.int32)[:, None]).astype(f32)
+    return jnp.dot(per_head, table, precision=lax.Precision.HIGHEST)
 
 
 def ranks(targets):
@@ -80,7 +86,7 @@
     return swapped * half + source // 2
 
 
-PIECES = 4
+PIECES = 8
 CHUNK = 640
 MESH = pl.DeviceIdType.MESH
 VMEM_LIMIT = 58 * 2**20
@@ -410,14 +416,6 @@
     in_page = jnp.arange(page_rows, dtype=jnp.int32)
     request_of, last_rows, ends = request_layout(page_counts[0], rows_here, page_rows)
 
-    page_items = slot_items(page_owners[:, 0], dp_count, PCAP)
-    page_source = jnp.where(
-        page_items[:, None] >= 0, page_items[:, None] * page_rows + in_page[None, :], -1
-    )
-    page_send = pick_rows(page_source.reshape(-1), keyval).reshape(
-        dp_count, PCAP * page_rows, -1
-    )
-
     grouped_local = conv_silu(group_rows, conv_groups, request_of)
     grouped = lax.all_gather(grouped_local, "tensor", axis=1, tiled=True)
     group_id = lax.axis_index("tensor") * heads_here // (HEADS // GROUPS)
@@ -426,14 +424,13 @@
     widths = jax.nn.softplus(step_rows.astype(f32) + step_bias)
     running = jnp.cumsum(-decay_rate * widths, 0)
     mixed = conv_silu(inner_rows, conv_inner, request_of)
-    values = mixed.astype(f32).reshape(rows_here, heads_here, HEAD_DIM)
 
     end_running = running[last_rows]
     end_of = jnp.zeros_like(running)
     for r in range(page_counts.shape[1]):
         end_of = jnp.where((request_of == r)[:, None], end_running[r][None, :], end_of)
     reach = jnp.exp(end_of - running) * widths
-    reached = (reach[:, :, None] * values).astype(bf16).reshape(rows_here, -1)
+    reached = (spread(reach) * mixed.astype(f32)).astype(bf16)
 
     slots = slot_items(owners[:, 0], dp_count, CAP)
     safe = jnp.maximum(slots, 0)
@@ -442,27 +439,56 @@
     span = jnp.arange(MOST_PAGES * page_rows, dtype=jnp.int32)
     used = (slots[:, None] >= 0) & (span[None, :] < (counts * page_rows)[:, None])
     source = jnp.where(used, first[:, None] + span[None, :], -1).reshape(-1)
-    value_send = pick_rows(source, reached).reshape(dp_count, CAP * span.shape[0], -1)
-    key_send = pick_rows(source, keys).reshape(dp_count, CAP * span.shape[0], -1)
     tail = jnp.where(
         slots[:, None] >= 0,
         last_rows[safe][:, None] - 2 + jnp.arange(3, dtype=jnp.int32)[None, :],
         -1,
     ).reshape(-1)
-    inner_send = pick_rows(tail, inner_rows).reshape(dp_count, CAP * 3, -1)
-    group_send = pick_rows(tail, group_rows).reshape(dp_count, CAP * 3, -1)
+    page_items = slot_items(page_owners[:, 0], dp_count, PCAP)
+    page_source = jnp.where(
+        page_items[:, None] >= 0, page_items[:, None] * page_rows + in_page[None, :], -1
+    ).reshape(-1)
+
+    def picked(rows, table):
+        return pick_rows(rows, table).reshape(dp_count, -1, table.shape[1])
+
+    def halves(items):
+        half = items.shape[2] // 2
+        return jnp.concatenate([items[:, :, :half], items[:, :, half:]], 1)
+
+    def whole(items):
+        half = items.shape[1] // 2
+        return jnp.concatenate([items[:, :half], items[:, half:]], 2)
 
     def swap(sent):
         return lax.all_to_all(sent, "dp", split_axis=0, concat_axis=0, tiled=True)
 
-    page_received = swap(page_send)
-    inner_received = swap(inner_send)
-    group_received = swap(group_send)
-    value_received = swap(value_send)
-    key_received = swap(key_send)
-
-    outputs = ssd_outputs(values, widths, running, keys, queries, request_of)
+    wide = w_inner.shape[1]
+    value_rows = CAP * span.shape[0]
+    tail_rows = CAP * 3
+    tails = picked(tail, jnp.concatenate([inner_rows, group_rows], 1))
+    inner_tail = jnp.pad(tails[:, :, :wide], ((0, 0), (0, 16 - tail_rows), (0, 0)))
+    group_tail = jnp.pad(halves(tails[:, :, wide:]), ((0, 0), (0, 16 - 2 * tail_rows), (0, 0)))
+    main_send = jnp.concatenate(
+        [
+            jnp.concatenate([picked(source, reached), halves(picked(page_source, keyval))], 2),
+            jnp.concatenate([inner_tail, group_tail], 2),
+        ],
+        1,
+    )
+    main = swap(main_send)
+    keys_after, _ = lax.optimization_barrier((keys, main_send))
+    key_received = swap(picked(source, keys_after))
+
+    weighted = (spread(widths) * mixed.astype(f32)).astype(bf16)
+    weighted = weighted.reshape(rows_here, heads_here, HEAD_DIM)
+    outputs = ssd_outputs(weighted, running, keys, queries, request_of)
     ssm_out = outputs.reshape(rows_here, heads_here * HEAD_DIM).astype(bf16)
+
+    value_received = main[:, :value_rows, :wide]
+    page_received = whole(main[:, :value_rows, wide:])
+    inner_received = main[:, value_rows : value_rows + tail_rows, :wide]
+    group_received = whole(main[:, value_rows : value_rows + 2 * tail_rows, wide:])
 
     slot_count = dp_count * CAP
     states = jnp.einsum(

time: 571 us -> 574 us (level)
  other arithmetic: 30.7 us -> 43.1 us
  starting transfers between devices: 22.3 us -> 10 us
    all_gather x1, waiting for transfers between devices: 0.01 us -> 16.6 us  [shards(): grouped = lax.all_gather(grouped_local, 'tensor', axis=1, tiled=True)]
    all_to_all x5 -> x2, waiting for transfers between devices: 84.1 us -> 71.5 us  [swap(): return lax.all_to_all(sent, 'dp', split_axis=0, concat_axis=0, tiled=True)]
    all_to_all x5 -> x2, starting transfers between devices: 22.1 us -> 9.99 us  [swap(): return lax.all_to_all(sent, 'dp', split_axis=0, concat_axis=0, tiled=True)]
    convert_element_type x1 -> x2, other arithmetic: 2.07 us -> 13.8 us  [conv_silu(): return jax.nn.silu(total).astype(bf16)]
    mul x3 -> x0, local copies, waits for them, and re-layouts: 8.96 us -> none  [the longest x2 7.91 us: shards(): reached = (reach[:, :, None] * values).astype(bf16).reshape(rows_here, -1)]
    slice x1 -> x9, local copies, waits for them, and re-layouts: 0.16 us -> 8.52 us  [the longest x1 4.81 us: shards(): value_received = main[:, :value_rows, :wide]]
    dot_general x0 -> x2, matrix products: none -> 7.87 us  [spread(): return jnp.dot(per_head, table, precision=lax.Precision.HIGHEST)]
    convert_element_type x3 -> x0, other arithmetic: 7.81 us -> none  [the longest x1 7.17 us: shards(): values = mixed.astype(f32).reshape(rows_here, heads_here, HEAD_DIM)]
  transfers between devices with their start and end apart: 6 -> 3, of which waited for: 3 -> 2; matrix products, arithmetic and copies ran while one was open for 13% -> 7% of each run, Pallas kernels for 0% -> 0%
where the time goes in v3:
time: 574 us; the launch traced here: 573 us
  Pallas kernels  342 us (60%)
  waiting for transfers between devices  88 us (15%)
  other arithmetic  43.1 us (8%)
  matrix products  36.9 us (6%)
  local copies, waits for them, and re-layouts  29.9 us (5%)
  between operations  14.4 us (3%)
  starting transfers between devices  10 us (2%)
  blocking collectives  8.31 us (1%)
    pallas_call x1, Pallas kernels, line_sums(): pl.pallas_call(functools.partial(line_kernel, count, widths), out_shape=j...  243 us
    pallas_call x1, Pallas kernels, share_blocks(): pl.pallas_call(functools.partial(share_kernel, count), out_shape=jax.Shap...  99 us
    all_to_all x2, waiting for transfers between devices, swap(): return lax.all_to_all(sent, 'dp', split_axis=0, concat_axis=0, tiled=True)  71.5 us
    all_gather x1, waiting for transfers between devices, shards(): grouped = lax.all_gather(grouped_local, 'tensor', axis=1, tiled=True)  16.6 us
    convert_element_type x2, other arithmetic, conv_silu(): return jax.nn.silu(total).astype(bf16)  13.8 us
  transfers between devices with their start and end apart: 3, of which 2 were waited for; matrix products, arithmetic and copies ran while one was open for 7% of the time, Pallas kernels for 0%

profile of v3, /device:TPU:0, one launch (start us, length us, event | category | flops | bytes accessed | tf_op | source)
XLA Modules:
  0.0 572.6 jit_solution(11820091344590300695)
XLA Ops:
  7.2 0.8 reduce-window.10
  8.0 0.9 convert_reduce_fusion.2
  8.9 0.7 iota_add_fusion.1
  9.6 0.1 select_reduce_fusion.1
  9.7 0.9 convert_reduce_fusion.1
  10.6 0.7 iota_add_fusion
  11.5 1.2 copy.35
  12.7 0.7 dynamic_slice.9
  13.4 3.5 fusion.8
  16.9 8.3 %psum.7 = f32[512,1]{0,1:T(1,128)S(1)} all-reduce(f32[512,1]{0,1:T(1,128)S(1)} %bitcast.103), channel_id=1, replica_groups=mesh['groups'=2,'dp'=4,'tensor'=4] {'tensor'}, use_global_device_ids=true, to_apply=%region_1.0 | all-reduce | flops 512 | bytes 4096 | tf_op jit(solution)/shard_map/psum | solution.py:394
  25.2 99.0 %shard_map.164.x_hbm = bf16[4,512,2048]{2,1,0:T(8,128)(2,1)} custom-call(bf16[512,2048]{1,0:T(8,128)(2,1)} %get-tuple-element.31.x_ref), custom_call_target="tpu_custom_call" | custom-call | tf_op jit(solution)/shard_map/pallas_call | solution.py:193
  124.2 0.9 pad.20.refs_2_
  125.1 242.9 %shard_map.165 = f32[512,3200]{1,0:T(8,128)} custom-call(bf16[4,512,2048]{2,1,0:T(8,128)(2,1)} %shard_map.164.x_hbm, bf16[2048,512]{1,0:T(8,128)(2,1)} %refs_0_.1, bf16[2048,512]{1,0:T(8,128)(2,1)} %refs_1_.1, bf16[2048,128]{1,0:T(8,128)(2,1)} %pad.20.refs_2_, bf16[2048,2048]{1,0:T(8,128)(2,1)} %refs_3_.1), custom_call_target="tpu_custom_call" | custom-call | flops 26843545600 | bytes 21495808 | tf_op jit(solution)/shard_map/pallas_call | solution.py:325
  368.0 3.5 multiply_convert_fusion.2
  371.5 1.3 fusion.76
  372.8 3.3 fusion.75
  376.2 0.6 gather_fusion.3
  377.0 2.9 convolution_convert_fusion.2
  379.9 0.9 reshape.372
  380.9 0.7 fusion.78
  381.6 0.5 neg.17
  382.1 1.2 gather_fusion.1
  383.3 1.2 gather_fusion
  384.5 0.6 pad_clamp_fusion
  385.2 0.7 select_n.170
  385.9 0.6 fusion.79
  386.5 0.8 broadcast_multiply_fusion
  387.3 0.7 copy.37
  388.1 2.3 reduce-window.11
  390.4 0.2 slice_reduce_fusion
  390.6 0.7 broadcast_add_fusion
  391.3 1.0 copy.38
  392.3 0.7 gather_fusion.2
  393.0 1.2 convolution_convert_fusion.3
  394.2 0.7 broadcast_multiply_fusion.1
  394.9 0.7 select_bitcast_fusion
  395.6 0.8 fusion.56
  396.4 9.9 %multiply_convert_fusion.3 = bf16[512,2048]{1,0:T(8,128)(2,1)S(1)} fusion(f32[509,2048]{1,0:T(8,128)} %bitcast.74, f32[510,2048]{1,0:T(8,128)} %bitcast.75, f32[511,2048]{1,0:T(8,128)} %bitcast.76, f32[2048]{0:T(1024)} %bitcast.97, f32[2048]{0:T(1024)} %bitcast.98, f32[2048]{0:T(1024)} %bitcast.96, f32[2048]{0:T(1024)} %bitcast.95, ...), kind=kLoop, calls=%fused_computation.24 | loop fusion | flops 16777216 | bytes 16762368 | tf_op jit(solution)/shard_map/convert_element_type | solution.py:33
  406.4 2.9 fusion.10
  409.4 2.4 convolution_convert_fusion.1
  411.8 4.8 fusion.6
  416.6 5.0 all-to-all-start
  421.7 0.9 fusion.80
  422.5 3.9 multiply_convert_fusion.6
  426.5 0.7 copy.39
  427.2 4.9 fusion.9
  432.1 2.9 copy.36
  435.1 0.2 fusion.19
  435.3 16.6 %all-gather.2.cloned.1.call-done = bf16[512,2048]{1,0:T(8,128)(2,1)} async-done(((bf16[512,512]{1,0:T(8,128)(2,1)}), bf16[512,2048]{1,0:T(8,128)(2,1)}) %all-gather.2.cloned.1.call-update) | async-done | bytes 2097168 | tf_op jit(solution)/shard_map/all_gather | solution.py:420
  451.8 1.0 constant_dynamic-slice_fusion
  452.8 1.3 fusion.16
  454.1 2.2 fusion.33
  456.4 71.5 %all-to-all-done = bf16[4,272,2304]{2,1,0:T(8,128)(2,1)} async-done(((bf16[4,272,2304]{2,1,0:T(8,128)(2,1)}), bf16[4,272,2304]{2,1,0:T(8,128)(2,1)}, u32[]{:S(2)}, u32[]{:S(2)}) %all-to-all-start) | async-done | bytes 5013536 | tf_op jit(solution)/shard_map/all_to_all | solution.py:464
  527.8 5.0 all-to-all-start.1
  532.8 11.0 %fusion.15 = bf16[32,64,512]{2,1,0:T(8,128)(2,1)} fusion(bf16[512,32,64]{0,2,1:T(8,128)(2,1)S(1)} %bitcast.87, f32[512,512]{1,0:T(8,128)} %fusion.33, f32[32,512]{1,0:T(8,128)S(1)} %copy-done.3, pred[512,512]{1,0:T(8,128)(4,1)S(1)} %fusion.19), kind=kOutput, calls=%fused_computation.32 | convolution fusion | flops 1108344832 | bytes 5570560 | tf_op jit(solution)/shard_map/hts,shd->thd/dot_general | solution.py:53
  543.9 3.9 copy.42
  547.8 0.8 fusion.74
  548.7 0.6 copy.44
  549.3 0.9 slice.209
  550.3 0.7 copy.43
  551.0 4.8 slice.208
  555.8 1.1 fusion.73
  556.9 0.8 pad_maximum_fusion
  557.7 8.0 %convolution_convert_fusion = bf16[8,2048,256]{2,1,0:T(8,128)(2,1)} fusion(bf16[8,128,2048]{2,1,0:T(8,128)(2,1)} %bitcast.80, bf16[8,128,256]{2,1,0:T(8,128)(2,1)S(1)} %bitcast.86), kind=kOutput, calls=%fused_computation.13 | convolution fusion | flops 1077936128 | bytes 13107200 | tf_op jit(solution)/shard_map/osc,osn->ocn/dot_general | solution.py:494
  (55 shorter events, 0.9 us)
Async XLA Ops:
  9.7 367.1 %copy-start.11 = (pred[8]{0:T(512)(128)(4,1)}, pred[8]{0:T(512)(128)(4,1)S(1)}, u32[]{:S(2)}) copy-start(pred[8]{0:T(512)(128)(4,1)S(1)} %add_compare_fusion.2) | copy-start | bytes 28
  376.2 5.4 copy-start.12
  376.2 7.2 %copy-start = (s32[1,8]{1,0:T(1,128)S(1)}, s32[1,8]{1,0:T(1,128)}, u32[]{:S(2)}) copy-start(s32[1,8]{1,0:T(1,128)} %param.23) | copy-start | bytes 100
  376.2 9.7 %copy-start.4 = (f32[4,2048]{1,0:T(4,128)S(1)}, f32[4,2048]{1,0:T(4,128)}, u32[]{:S(2)}) copy-start(f32[4,2048]{1,0:T(4,128)} %param.19) | copy-start | bytes 98308
  376.2 10.3 %copy-start.7 = (f32[32]{0:T(128)S(1)}, f32[32]{0:T(128)}, u32[]{:S(2)}) copy-start(f32[32]{0:T(128)} %param.22) | copy-start | bytes 388
  380.9 5.0 copy-start.2
  395.6 13.8 %copy-start.9 = (s32[1024]{0:T(1024)}, s32[1024]{0:T(1024)S(1)}, u32[]{:S(2)}) copy-start(s32[1024]{0:T(1024)S(1)} %select_bitcast_fusion) | copy-start | bytes 12292
  396.4 9.9 %copy-start.5 = (pred[512]{0:T(512)(128)(4,1)}, pred[512]{0:T(512)(128)(4,1)S(1)}, u32[]{:S(2)}) copy-start(pred[512]{0:T(512)(128)(4,1)S(1)} %get-tuple-element.61) | copy-start | bytes 1540
  396.4 10.0 %copy-start.6 = (pred[512]{0:T(512)(128)(4,1)}, pred[512]{0:T(512)(128)(4,1)S(1)}, u32[]{:S(2)}) copy-start(pred[512]{0:T(512)(128)(4,1)S(1)} %get-tuple-element.62) | copy-start | bytes 1540
  396.4 10.0 %copy-start.8 = (f32[32]{0:T(128)S(1)}, f32[32]{0:T(128)}, u32[]{:S(2)}) copy-start(f32[32]{0:T(128)} %param.22) | copy-start | bytes 388
  406.4 5.4 copy-start.1
  409.4 2.4 slice-start
  416.6 111.2 %all-to-all-start = ((bf16[4,272,2304]{2,1,0:T(8,128)(2,1)}), bf16[4,272,2304]{2,1,0:T(8,128)(2,1)}, u32[]{:S(2)}, u32[]{:S(2)}) async-start(bf16[4,272,2304]{2,1,0:T(8,128)(2,1)} %fusion.6), calls=%async_computation | async-start | bytes 10027008 | tf_op jit(solution)/shard_map/all_to_all | solution.py:464
  421.6 30.2 %all-gather.2.cloned.1.call-start = ((), (), s32[]{:S(2)}) async-start(), calls=%async_computation.2 | async-start | bytes 2621440 | tf_op jit(solution)/shard_map/all_gather | solution.py:420
  427.2 25.6 %copy-start.10 = (s32[1024]{0:T(1024)S(1)}, s32[1024]{0:T(1024)}, u32[]{:S(2)}) copy-start(s32[1024]{0:T(1024)} %copy-done.9) | copy-start | bytes 12292
  432.1 100.7 %copy-start.3 = (f32[32,512]{1,0:T(8,128)S(1)}, f32[32,512]{1,0:T(8,128)}, u32[]{:S(2)}) copy-start(f32[32,512]{1,0:T(8,128)} %copy.39) | copy-start | bytes 196612
  527.8 29.9 %all-to-all-start.1 = ((bf16[4,256,256]{2,1,0:T(8,128)(2,1)}), bf16[4,256,256]{2,1,0:T(8,128)(2,1)S(1)}, u32[]{:S(2)}, u32[]{:S(2)}) async-start(bf16[4,256,256]{2,1,0:T(8,128)(2,1)} %bitcast.35), calls=%async_computation.1 | async-start | bytes 1048576 | tf_op jit(solution)/shard_map/all_to_all | solution.py:464
Sparse Core Ops, SparseCore 0:
  426.6 25.2 all-gather.1

commit v4 on v3

--- a/solution.py
+++ b/solution.py
@@ -477,13 +477,14 @@
         1,
     )
     main = swap(main_send)
-    keys_after, _ = lax.optimization_barrier((keys, main_send))
-    key_received = swap(picked(source, keys_after))
 
     weighted = (spread(widths) * mixed.astype(f32)).astype(bf16)
     weighted = weighted.reshape(rows_here, heads_here, HEAD_DIM)
     outputs = ssd_outputs(weighted, running, keys, queries, request_of)
     ssm_out = outputs.reshape(rows_here, heads_here * HEAD_DIM).astype(bf16)
+
+    keys_after, ssm_out = lax.optimization_barrier((keys, ssm_out))
+    key_received = swap(picked(source, keys_after))
 
     value_received = main[:, :value_rows, :wide]
     page_received = whole(main[:, :value_rows, wide:])

time: 574 us -> 563 us (0.981)
  waiting for transfers between devices: 88 us -> 78.9 us
    all_to_all x2, waiting for transfers between devices: 71.5 us -> 62.3 us  [swap(): return lax.all_to_all(sent, 'dp', split_axis=0, concat_axis=0, tiled=True)]
where the time goes in v4:
time: 563 us; the launch traced here: 562 us
  Pallas kernels  342 us (61%)
  waiting for transfers between devices  78.9 us (14%)
  other arithmetic  43.1 us (8%)
  matrix products  35.1 us (6%)
  local copies, waits for them, and re-layouts  29.9 us (5%)
  between operations  14.4 us (3%)
  starting transfers between devices  10 us (2%)
  blocking collectives  8.31 us (1%)
    pallas_call x1, Pallas kernels, line_sums(): pl.pallas_call(functools.partial(line_kernel, count, widths), out_shape=j...  243 us
    pallas_call x1, Pallas kernels, share_blocks(): pl.pallas_call(functools.partial(share_kernel, count), out_shape=jax.Shap...  99 us
    all_to_all x2, waiting for transfers between devices, swap(): return lax.all_to_all(sent, 'dp', split_axis=0, concat_axis=0, tiled=True)  62.3 us
    all_gather x1, waiting for transfers between devices, shards(): grouped = lax.all_gather(grouped_local, 'tensor', axis=1, tiled=True)  16.6 us
    convert_element_type x2, other arithmetic, conv_silu(): return jax.nn.silu(total).astype(bf16)  13.8 us
  transfers between devices with their start and end apart: 3, of which 2 were waited for; matrix products, arithmetic and copies ran while one was open for 7% of the time, Pallas kernels for 0%

profile of v4, /device:TPU:0, one launch (start us, length us, event | category | flops | bytes accessed | tf_op | source)
XLA Modules:
  0.0 561.5 jit_solution(5256629308920664226)
XLA Ops:
  7.2 0.8 reduce-window.10
  8.0 0.9 convert_reduce_fusion.2
  8.9 0.7 iota_add_fusion.1
  9.6 0.1 select_reduce_fusion.1
  9.7 0.9 convert_reduce_fusion.1
  10.6 0.7 iota_add_fusion
  11.5 1.2 copy.35
  12.7 0.7 dynamic_slice.9
  13.4 3.5 fusion.8
  16.9 8.3 %psum.7 = f32[512,1]{0,1:T(1,128)S(1)} all-reduce(f32[512,1]{0,1:T(1,128)S(1)} %bitcast.103), channel_id=1, replica_groups=mesh['groups'=2,'dp'=4,'tensor'=4] {'tensor'}, use_global_device_ids=true, to_apply=%region_1.0 | all-reduce | flops 512 | bytes 4096 | tf_op jit(solution)/shard_map/psum | solution.py:394
  25.2 99.0 %shard_map.164.x_hbm = bf16[4,512,2048]{2,1,0:T(8,128)(2,1)} custom-call(bf16[512,2048]{1,0:T(8,128)(2,1)} %get-tuple-element.33.x_ref), custom_call_target="tpu_custom_call" | custom-call | tf_op jit(solution)/shard_map/pallas_call | solution.py:193
  124.2 0.9 pad.20.refs_2_
  125.1 242.9 %shard_map.165 = f32[512,3200]{1,0:T(8,128)} custom-call(bf16[4,512,2048]{2,1,0:T(8,128)(2,1)} %shard_map.164.x_hbm, bf16[2048,512]{1,0:T(8,128)(2,1)} %refs_0_.1, bf16[2048,512]{1,0:T(8,128)(2,1)} %refs_1_.1, bf16[2048,128]{1,0:T(8,128)(2,1)} %pad.20.refs_2_, bf16[2048,2048]{1,0:T(8,128)(2,1)} %refs_3_.1), custom_call_target="tpu_custom_call" | custom-call | flops 26843545600 | bytes 21495808 | tf_op jit(solution)/shard_map/pallas_call | solution.py:325
  368.0 3.5 multiply_convert_fusion.2
  371.5 1.3 fusion.76
  372.8 3.3 fusion.75
  376.2 0.6 gather_fusion.3
  377.0 2.9 convolution_convert_fusion.2
  379.9 0.9 reshape.372
  380.9 0.7 fusion.78
  381.6 0.5 neg.18
  382.1 1.2 gather_fusion.1
  383.3 1.2 gather_fusion
  384.5 0.6 pad_clamp_fusion
  385.2 0.7 select_n.170
  385.9 0.6 fusion.79
  386.5 0.8 broadcast_multiply_fusion
  387.3 0.7 copy.37
  388.1 2.3 reduce-window.11
  390.4 0.2 slice_reduce_fusion
  390.6 0.7 broadcast_add_fusion
  391.3 1.0 copy.38
  392.3 0.7 gather_fusion.2
  393.0 1.2 convolution_convert_fusion.3
  394.2 0.7 broadcast_multiply_fusion.1
  394.9 0.7 select_bitcast_fusion
  395.6 0.8 fusion.56
  396.4 9.9 %multiply_convert_fusion.3 = bf16[512,2048]{1,0:T(8,128)(2,1)S(1)} fusion(f32[509,2048]{1,0:T(8,128)} %bitcast.74, f32[510,2048]{1,0:T(8,128)} %bitcast.75, f32[511,2048]{1,0:T(8,128)} %bitcast.76, f32[2048]{0:T(1024)} %bitcast.97, f32[2048]{0:T(1024)} %bitcast.98, f32[2048]{0:T(1024)} %bitcast.96, f32[2048]{0:T(1024)} %bitcast.95, ...), kind=kLoop, calls=%fused_computation.24 | loop fusion | flops 16777216 | bytes 16762368 | tf_op jit(solution)/shard_map/convert_element_type | solution.py:33
  406.4 2.9 fusion.10
  409.4 2.4 convolution_convert_fusion.1
  411.8 4.8 fusion.6
  416.6 5.0 all-to-all-start
  421.7 0.9 fusion.80
  422.5 3.9 multiply_convert_fusion.6
  426.5 0.7 copy.39
  427.2 4.9 fusion.9
  432.1 2.9 copy.36
  435.1 0.2 fusion.19
  435.3 16.6 %all-gather.2.cloned.1.call-done = bf16[512,2048]{1,0:T(8,128)(2,1)} async-done(((bf16[512,512]{1,0:T(8,128)(2,1)}), bf16[512,2048]{1,0:T(8,128)(2,1)}) %all-gather.2.cloned.1.call-update) | async-done | bytes 2097168 | tf_op jit(solution)/shard_map/all_gather | solution.py:420
  451.8 1.0 constant_dynamic-slice_fusion
  452.8 1.3 fusion.33
  454.1 10.1 %fusion.15 = bf16[32,64,512]{2,1,0:T(8,128)(2,1)} fusion(bf16[512,32,64]{0,2,1:T(8,128)(2,1)S(1)} %bitcast.87, f32[512,512]{1,0:T(8,128)S(1)} %fusion.33, f32[32,512]{1,0:T(8,128)S(1)} %copy-done.3, pred[512,512]{1,0:T(8,128)(4,1)S(1)} %fusion.19), kind=kOutput, calls=%fused_computation.32 | convolution fusion | flops 1108344832 | bytes 5570560 | tf_op jit(solution)/shard_map/hts,shd->thd/dot_general | solution.py:53
  464.2 1.3 fusion.16
  465.6 62.3 %all-to-all-done = bf16[4,272,2304]{2,1,0:T(8,128)(2,1)} async-done(((bf16[4,272,2304]{2,1,0:T(8,128)(2,1)}), bf16[4,272,2304]{2,1,0:T(8,128)(2,1)}, u32[]{:S(2)}, u32[]{:S(2)}) %all-to-all-start) | async-done | bytes 5013536 | tf_op jit(solution)/shard_map/all_to_all | solution.py:464
  527.8 5.0 all-to-all-start.1
  532.8 3.9 copy.42
  536.7 0.8 fusion.74
  537.6 0.6 copy.44
  538.2 0.9 slice.209
  539.2 0.7 copy.43
  540.0 4.8 slice.208
  544.8 1.1 fusion.73
  545.9 0.8 pad_maximum_fusion
  546.7 8.0 %convolution_convert_fusion = bf16[8,2048,256]{2,1,0:T(8,128)(2,1)} fusion(bf16[8,128,2048]{2,1,0:T(8,128)(2,1)} %bitcast.80, bf16[8,128,256]{2,1,0:T(8,128)(2,1)S(1)} %bitcast.86), kind=kOutput, calls=%fused_computation.13 | convolution fusion | flops 1077936128 | bytes 13107200 | tf_op jit(solution)/shard_map/osc,osn->ocn/dot_general | solution.py:495
  (55 shorter events, 0.9 us)
Async XLA Ops:
  9.7 367.1 %copy-start.11 = (pred[8]{0:T(512)(128)(4,1)}, pred[8]{0:T(512)(128)(4,1)S(1)}, u32[]{:S(2)}) copy-start(pred[8]{0:T(512)(128)(4,1)S(1)} %add_compare_fusion.2) | copy-start | bytes 28
  376.2 5.4 copy-start.12
  376.2 7.2 %copy-start = (s32[1,8]{1,0:T(1,128)S(1)}, s32[1,8]{1,0:T(1,128)}, u32[]{:S(2)}) copy-start(s32[1,8]{1,0:T(1,128)} %param.23) | copy-start | bytes 100
  376.2 9.7 %copy-start.4 = (f32[4,2048]{1,0:T(4,128)S(1)}, f32[4,2048]{1,0:T(4,128)}, u32[]{:S(2)}) copy-start(f32[4,2048]{1,0:T(4,128)} %param.19) | copy-start | bytes 98308
  376.2 10.3 %copy-start.7 = (f32[32]{0:T(128)S(1)}, f32[32]{0:T(128)}, u32[]{:S(2)}) copy-start(f32[32]{0:T(128)} %param.22) | copy-start | bytes 388
  380.9 5.0 copy-start.2
  395.6 13.8 %copy-start.9 = (s32[1024]{0:T(1024)}, s32[1024]{0:T(1024)S(1)}, u32[]{:S(2)}) copy-start(s32[1024]{0:T(1024)S(1)} %select_bitcast_fusion) | copy-start | bytes 12292
  396.4 9.9 %copy-start.5 = (pred[512]{0:T(512)(128)(4,1)}, pred[512]{0:T(512)(128)(4,1)S(1)}, u32[]{:S(2)}) copy-start(pred[512]{0:T(512)(128)(4,1)S(1)} %get-tuple-element.63) | copy-start | bytes 1540
  396.4 10.0 %copy-start.6 = (pred[512]{0:T(512)(128)(4,1)}, pred[512]{0:T(512)(128)(4,1)S(1)}, u32[]{:S(2)}) copy-start(pred[512]{0:T(512)(128)(4,1)S(1)} %get-tuple-element.64) | copy-start | bytes 1540
  396.4 10.0 %copy-start.8 = (f32[32]{0:T(128)S(1)}, f32[32]{0:T(128)}, u32[]{:S(2)}) copy-start(f32[32]{0:T(128)} %param.22) | copy-start | bytes 388
  406.4 5.4 copy-start.1
  409.4 2.4 slice-start
  416.6 111.2 %all-to-all-start = ((bf16[4,272,2304]{2,1,0:T(8,128)(2,1)}), bf16[4,272,2304]{2,1,0:T(8,128)(2,1)}, u32[]{:S(2)}, u32[]{:S(2)}) async-start(bf16[4,272,2304]{2,1,0:T(8,128)(2,1)} %fusion.6), calls=%async_computation | async-start | bytes 10027008 | tf_op jit(solution)/shard_map/all_to_all | solution.py:464
  421.6 30.2 %all-gather.2.cloned.1.call-start = ((), (), s32[]{:S(2)}) async-start(), calls=%async_computation.2 | async-start | bytes 2621440 | tf_op jit(solution)/shard_map/all_gather | solution.py:420
  432.1 21.9 %copy-start.3 = (f32[32,512]{1,0:T(8,128)S(1)}, f32[32,512]{1,0:T(8,128)}, u32[]{:S(2)}) copy-start(f32[32,512]{1,0:T(8,128)} %copy.39) | copy-start | bytes 196612
  454.1 10.1 %copy-start.10 = (s32[1024]{0:T(1024)S(1)}, s32[1024]{0:T(1024)}, u32[]{:S(2)}) copy-start(s32[1024]{0:T(1024)} %copy-done.9) | copy-start | bytes 12292
  527.8 18.8 %all-to-all-start.1 = ((bf16[4,256,256]{2,1,0:T(8,128)(2,1)}), bf16[4,256,256]{2,1,0:T(8,128)(2,1)S(1)}, u32[]{:S(2)}, u32[]{:S(2)}) async-start(bf16[4,256,256]{2,1,0:T(8,128)(2,1)} %bitcast.35), calls=%async_computation.1 | async-start | bytes 1048576 | tf_op jit(solution)/shard_map/all_to_all | solution.py:464
Sparse Core Ops, SparseCore 0:
  426.6 25.2 all-gather.1
